TPU v7x, 32 devices: a whole 2x2x4 slice. The times are simulated.
32 devices in a mesh: rep: 2 (over x), adp: 16 (over z, y, core).
Axes of the slice: x: 2, y: 2, z: 4, core: 2. Of those that a mesh axis runs over, the one named last changes fastest.
Arguments:
- tokens: bfloat16 [768, 8192], P('rep', 'adp'), parts along dimension 0, may hold values from -6 to 6
- request_adapter: int32 [768, 1], P('rep'), parts along dimension 0, may hold values from 0 to 15
- adapter_storage_slot: int32 [16], replicated, may hold values from 0 to 15, each once
- cache_length: int32 [768], P(('rep', 'adp')), parts along dimension 0, may hold values from 2 to 128, as said below
- query_weight: bfloat16 [8192, 8192], P(None, 'adp'), may hold values from -0.0625 to 0.0625
- adapter_down_maps: bfloat16 [16, 8192, 64], P('adp'), may hold values from -0.0625 to 0.0625
- adapter_up_maps: bfloat16 [16, 8192, 64], P('adp'), may hold values from -0.75 to 0.75
- key_cache: bfloat16 [8, 768, 128, 128], P(None, ('rep', 'adp')), parts along dimension 1, may hold values from -250 to 250
- value_cache: bfloat16 [8, 768, 128, 128], P(None, ('rep', 'adp')), parts along dimension 1, may hold values from -6 to 6
- new_token_key: bfloat16 [768, 1024], P(('rep', 'adp')), parts along dimension 0, may hold values from -6 to 6
- new_token_value: bfloat16 [768, 1024], P(('rep', 'adp')), parts along dimension 0, may hold values from -6 to 6
- output_weight: bfloat16 [8192, 8192], P('adp'), may hold values from -0.09375 to 0.09375
Outputs:
- attn_out: bfloat16 [768, 8192], P('rep', 'adp'), parts along dimension 0
There are 2 independent parts, one for each index of `rep`. A program takes and returns all parts, laid end to end along the dimension named above; an argument that names none is the same for every part. Nothing has to cross between parts.
Inputs may be any that keep to these rules, and one draw needn't show every extreme that they name: `request_adapter`: every adapter is named by some request of a group. `adapter_storage_slot`: each adapter id has its own slot. `cache_length`: some request holds exactly 128 positions.
All inputs are finite; a program needn't handle non-finite values.
Results may differ from a plain program's by a relative error of at most 0.011.
Values may be sent and summed in bfloat16 or wider, within the bound.
No kernel may reach another device: no remote copies, remote signals or barrier semaphores. Data moves between devices by JAX's collectives and lax.ppermute only.
A program may use at most 128 MiB of HBM per device.

v0:
```python
import jax
import jax.numpy as jnp
from jax import lax
from jax.experimental import pallas as pl
from jax.experimental.pallas import tpu as pltpu
from jax.sharding import Mesh
from jax.sharding import PartitionSpec as P

HEADS = 64
HEAD_DIM = 128
ADP = ("z", "y", "core")
GATHERED = ((0, 0), (0, 1), (3, 0), (1, 0), (3, 1), (1, 1), (2, 0), (2, 1))
NT = (((1,), (1,)), ((), ()))
VMEM_LIMIT = 56 << 20
QUICK = pl.CostEstimate(flops=1, bytes_accessed=1, transcendentals=0)


def project_kernel(places, first, count, *refs):
    blocks, w_own, w_other, a_own, a_other = (refs[i * count : (i + 1) * count] for i in range(5))
    ins, outs = refs[5 * count : -3], refs[-3:]
    first_core = places[0] % 2 == 0
    sums = [ref[...] for ref in ins[:3]]
    for i in range(count):
        x = blocks[i][...]
        own, other = a_own[i][0], a_other[i][0]
        pair = jnp.concatenate(
            [jnp.where(first_core, own, other), jnp.where(first_core, other, own)], axis=0
        )
        parts = (
            jnp.dot(x, w_own[i][...], preferred_element_type=jnp.float32),
            jnp.dot(x, w_other[i][...], preferred_element_type=jnp.float32),
            lax.dot_general(x, pair, NT, preferred_element_type=jnp.float32),
        )
        sums = [total + part for total, part in zip(sums, parts)] if sums else parts
    outs[0][...], outs[1][...] = sums[:2]
    low = sums[2]
    if ins:
        slot = ins[3][...]
        rank = low.shape[1] // 2
        mine = places[0] - places[0] % 2
        low = jnp.where(slot == mine, low[:, :rank], 0.0) + jnp.where(
            slot == mine + 1, low[:, rank:], 0.0
        )
        half = low.shape[0] // 2
        low = jnp.concatenate([low[:half], low[half:]], axis=1)
    outs[2][...] = low


def project(places, first, blocks, weight, weight_other, down, down_other, rest):
    count = len(blocks)
    rows, width = blocks[0].shape
    cols, rank = weight.shape[1], down.shape[1]
    flat = lambda shape: pl.BlockSpec(shape, lambda j, p: (0, 0))
    low_rows = rows // 2 if rest else rows
    shapes = [(rows, cols), (rows, cols), (low_rows, 2 * rank)]
    weights = [pl.BlockSpec((width, cols), lambda j, p, i=i: (p[first + i], 0)) for i in range(count)]
    maps = [
        pl.BlockSpec((1, rank, width), lambda j, p, i=i: (0, 0, p[first + i])) for i in range(count)
    ]

    def kernel(places, *refs):
        project_kernel(places, first, count, *refs)

    return pl.pallas_call(
        kernel,
        grid_spec=pltpu.PrefetchScalarGridSpec(
            num_scalar_prefetch=1,
            grid=(1,),
            in_specs=[flat((rows, width))] * count
            + weights * 2
            + maps * 2
            + [flat(array.shape) for array in rest],
            out_specs=[flat(shape) for shape in shapes],
        ),
        out_shape=[jax.ShapeDtypeStruct(shape, jnp.float32) for shape in shapes],
        compiler_params=pltpu.CompilerParams(vmem_limit_bytes=VMEM_LIMIT),
        cost_estimate=QUICK,
    )(
        places,
        *blocks,
        *[weight] * count,
        *[weight_other] * count,
        *[down] * count,
        *[down_other] * count,
        *rest,
    )


def query_kernel(half, own, received, low, slot, up_own, up_other, out):
    step = pl.program_id(0)
    lanes = low.shape[1]
    rank = lanes // 2
    part = rank // 2
    depth = up_own.shape[0]
    shape = (lanes, depth)
    lane = lax.broadcasted_iota(jnp.int32, shape, 1) % part
    row = lax.broadcasted_iota(jnp.int32, shape, 0)
    owner = lax.broadcasted_iota(jnp.int32, (own.shape[0], depth), 1) // part
    live = slot[...] == owner
    total = own[...] + received[...]
    for h, up in ((half[0], up_own), (1 - half[0], up_other)):
        copies = (row == lane + rank * step + part * h).astype(jnp.bfloat16)
        spread = jnp.dot(low[...], copies, preferred_element_type=jnp.float32)
        spread = jnp.where(live, spread, 0.0).astype(jnp.bfloat16)
        total += jnp.dot(spread, up[...], preferred_element_type=jnp.float32)
    out[...] = (total * HEAD_DIM ** (-0.5)).astype(out.dtype)


def make_query(half, own, received, low, slot, up_own, up_other):
    rows, cols = own.shape
    tile = rows // 2
    depth = up_own.shape[0]
    by_rows = lambda width: pl.BlockSpec((tile, width), lambda j, h: (j, 0))
    whole = lambda array: pl.BlockSpec(array.shape, lambda j, h: (0, 0))
    return pl.pallas_call(
        query_kernel,
        grid_spec=pltpu.PrefetchScalarGridSpec(
            num_scalar_prefetch=1,
            grid=(2,),
            in_specs=[
                by_rows(cols),
                by_rows(received.shape[1]),
                whole(low),
                by_rows(1),
                whole(up_own),
                whole(up_other),
            ],
            out_specs=by_rows(cols),
        ),
        out_shape=jax.ShapeDtypeStruct((rows, cols), jnp.bfloat16),
        compiler_params=pltpu.CompilerParams(vmem_limit_bytes=VMEM_LIMIT),
        cost_estimate=QUICK,
    )(half, own, received, low, slot, up_own, up_other)


def output_kernel(places, count, own, other, *refs):
    for w_own, w_other, out in zip(refs[:count], refs[count : 2 * count], refs[2 * count :]):
        total = jnp.dot(own[...], w_own[...], preferred_element_type=jnp.float32)
        total += jnp.dot(other[...], w_other[...], preferred_element_type=jnp.float32)
        out[...] = total.astype(out.dtype)


def output_partial(places, first, count, own, other, weight, weight_other, width):
    rows, depth = own.shape
    tile = width // 2 if width % 256 == 0 else width
    steps = width // tile
    whole = pl.BlockSpec((rows, depth), lambda j, p: (0, 0))
    weights = [
        pl.BlockSpec((depth, tile), lambda j, p, i=i: (0, p[first + i] * steps + j))
        for i in range(count)
    ]

    def kernel(places, *refs):
        output_kernel(places, count, *refs)

    return pl.pallas_call(
        kernel,
        grid_spec=pltpu.PrefetchScalarGridSpec(
            num_scalar_prefetch=1,
            grid=(steps,),
            in_specs=[whole, whole] + weights * 2,
            out_specs=[pl.BlockSpec((rows, tile), lambda j, p: (0, j))] * count,
        ),
        out_shape=[jax.ShapeDtypeStruct((rows, width), jnp.bfloat16)] * count,
        compiler_params=pltpu.CompilerParams(vmem_limit_bytes=VMEM_LIMIT),
        cost_estimate=QUICK,
    )(places, own, other, *[weight] * count, *[weight_other] * count)


def attention(query, cache_length, key_cache, value_cache, k_new, v_new):
    local_reqs = query.shape[0]
    kv_count, _, span, dim = key_cache.shape
    group = HEADS // kv_count
    query = query.reshape(local_reqs, kv_count, group, dim)
    k_new = k_new.reshape(local_reqs, kv_count, dim)
    v_new = v_new.reshape(local_reqs, kv_count, dim)
    live = (jnp.arange(span)[None, :] < cache_length[:, None])[None, :, None, :]
    scores = jnp.einsum("rkge,krje->krgj", query, key_cache, preferred_element_type=jnp.float32)
    fresh = jnp.einsum("rkge,rke->krg", query, k_new, preferred_element_type=jnp.float32)
    scores = jnp.where(live, scores, -jnp.inf)
    top = jnp.maximum(jnp.max(scores, axis=3), fresh)
    expd = jnp.where(live, jnp.exp(scores - top[:, :, :, None]), 0.0)
    expf = jnp.exp(fresh - top)
    total = jnp.sum(expd, axis=3) + expf
    probs = (expd / total[:, :, :, None]).astype(jnp.bfloat16)
    probf = (expf / total).astype(jnp.bfloat16)
    context = jnp.einsum("krgj,krje->rkge", probs, value_cache, preferred_element_type=jnp.float32)
    fresh_part = jnp.einsum("krg,rke->rkge", probf.astype(jnp.float32), v_new.astype(jnp.float32))
    return (context + fresh_part).astype(jnp.bfloat16).reshape(local_reqs, HEADS * dim)


def shift(value, axis, by):
    size = lax.axis_size(axis)
    return lax.ppermute(value, axis, [(i, (i + by) % size) for i in range(size)])


def after(value, *others):
    return lax.optimization_barrier((value, *others))[0]


def gathered_chips():
    layers, sides = lax.axis_size("z"), lax.axis_size("y")
    z, y = lax.axis_index("z"), lax.axis_index("y")
    steps = GATHERED
    if layers != 4 or sides != 2:
        steps = [(-k, side) for k in range(layers) for side in range(sides)]
    return [((z + k) % layers) * sides + (y + side) % sides for k, side in steps]


def gather_features(tokens, down_other, up, begin):
    layers, sides = lax.axis_size("z"), lax.axis_size("y")
    z = lax.axis_index("z")
    if layers != 4 or sides != 2:
        blocks = [shift(tokens, "z", k) if k else tokens for k in range(layers)]
        blocks = [[block, shift(block, "y", 1)][:sides] for block in blocks]
        blocks = [block for pair in blocks for block in pair]
        return begin(blocks[:-1]), blocks[-1:], up
    side = shift(tokens, "y", 1)
    below, above = shift(tokens, "z", 1), shift(tokens, "z", 3)
    below, side, _ = lax.optimization_barrier((below, side, down_other))
    below_side = shift(below, "y", 1)
    from_below = lax.ppermute(below, "z", [(1, 2), (2, 3)])
    above_side = shift(above, "y", 1)
    from_above = lax.ppermute(above, "z", [(2, 1), (1, 0)])
    sums = begin([tokens, side, below, above])
    two = jnp.where(z >= 2, from_below, from_above)
    two, _, up, sums = lax.optimization_barrier((two, below_side, up, sums))
    return sums, [below_side, above_side, two, shift(two, "y", 1)], up


def scatter_layers(parts):
    layers = lax.axis_size("z")
    wide = lambda value: value.astype(jnp.float32)
    narrow = lambda value: value.astype(jnp.bfloat16)
    if layers != 4:
        return sum([wide(shift(narrow(parts[k]), "z", k)) for k in range(1, layers)], parts[0])
    two = narrow(parts[2])
    up = lax.ppermute(two, "z", [(0, 1), (1, 2)])
    down = lax.ppermute(two, "z", [(3, 2), (2, 1)])
    above = shift(narrow(parts[1] + wide(up)), "z", 1)
    below = shift(narrow(parts[3] + wide(down)), "z", 3)
    return parts[0] + wide(above) + wide(below)


def shards(
    tokens,
    request_adapter,
    adapter_storage_slot,
    cache_length,
    query_weight,
    adapter_down_maps,
    adapter_up_maps,
    key_cache,
    value_cache,
    new_token_key,
    new_token_value,
    output_weight,
):
    layers, sides = lax.axis_size("z"), lax.axis_size("y")
    z, y, core = lax.axis_index("z"), lax.axis_index("y"), lax.axis_index("core")
    rows, width = tokens.shape
    total_adapters = adapter_storage_slot.shape[0]
    rank = adapter_down_maps.shape[2]
    depth = output_weight.shape[0]
    chips_of = lambda layer: [
        (layer % layers) * sides + (y + side) % sides for side in range(sides)
    ]

    down = jnp.swapaxes(adapter_down_maps, 1, 2)
    down_other = shift(down, "core", 1)
    query_weight_other = shift(query_weight, "core", 1)

    ids = request_adapter[:, 0]
    numbers = jnp.arange(total_adapters, dtype=jnp.int32)
    slot = jnp.sum(
        jnp.where(ids[:, None] == numbers[None, :], adapter_storage_slot[None, :], 0), axis=1
    )[:, None]

    out_order = [2, 1, 3, 0] if layers == 4 else list(range(1, layers)) + [0]
    out_keys = [(k, side) for k in out_order for side in reversed(range(sides))]
    chips = gathered_chips()
    out_first = len(chips)
    chips += [chips_of(z + k)[side] for k, side in out_keys]
    places = jnp.stack([2 * chip + core for chip in chips]).astype(jnp.int32)

    weights = query_weight, query_weight_other, down, down_other
    half = lax.axis_index("rep") % 2
    up = jnp.swapaxes(adapter_up_maps, 1, 2)[0]
    up = lax.dynamic_slice_in_dim(up, half * (rank // 2), rank // 2, 0)
    up = lax.all_to_all(up, ADP, split_axis=1, concat_axis=0, tiled=True)
    sums, blocks, up = gather_features(
        tokens, down_other, up, lambda blocks: project(places, 0, blocks, *weights, ())
    )
    up_other = lax.ppermute(up, "rep", [(i, i ^ 1) for i in range(lax.axis_size("rep"))])

    own, sent, low = project(places, out_first - len(blocks), blocks, *weights, (*sums, slot))

    low = (low + shift(low, "core", 1)).astype(jnp.bfloat16)
    received = shift(sent, "core", 1)
    if sides == 2:
        low = low + shift(low, "y", 1)
    low, received, up_other = lax.optimization_barrier((low, received, up_other))
    low = sum([shift(low, "z", k) for k in range(1, layers)], low)

    query = make_query(half.astype(jnp.int32).reshape(1), own, received, low, slot, up, up_other)
    output_weight_other = shift(after(output_weight, query), "core", 1)
    query_local = lax.all_to_all(query, ADP, split_axis=0, concat_axis=1, tiled=True)

    context = attention(
        query_local, cache_length, key_cache, value_cache, new_token_key, new_token_value
    )
    context = jnp.swapaxes(context.reshape(context.shape[0], -1, depth), 0, 1)
    context = lax.all_to_all(context, ADP, split_axis=0, concat_axis=0, tiled=True)
    context = context.reshape(rows, depth)
    context_other = shift(context, "core", 1)

    made = {}
    for first, count in ((0, 1), (1, len(out_keys) - 1)):
        outs = output_partial(
            places,
            out_first + first,
            count,
            context,
            context_other,
            output_weight,
            output_weight_other,
            width,
        )
        made.update(zip(out_keys[first : first + count], outs))
    other_side = {k: shift(made[k, 1], "y", 1) for k in out_order if sides == 2}
    parts = [None] * layers
    for k in out_order:
        parts[k] = after(made[k, 0], made[out_keys[-1]]).astype(jnp.float32)
        if sides == 2:
            parts[k] = parts[k] + other_side[k].astype(jnp.float32)
    return scatter_layers(parts).astype(jnp.bfloat16)


def solution(mesh):
    reps, adp = mesh.shape["rep"], mesh.shape["adp"]
    sides = 2 if adp == 16 else 1
    mesh = Mesh(mesh.devices.reshape(reps, adp // (2 * sides), sides, 2), ("rep",) + ADP)
    in_specs = (
        P("rep", ADP),
        P("rep", None),
        P(),
        P(("rep",) + ADP),
        P(None, ADP),
        P(ADP, None, None),
        P(ADP, None, None),
        P(None, ("rep",) + ADP, None, None),
        P(None, ("rep",) + ADP, None, None),
        P(("rep",) + ADP, None),
        P(("rep",) + ADP, None),
        P(ADP, None),
    )
    return jax.shard_map(
        shards, mesh=mesh, in_specs=in_specs, out_specs=P("rep", ADP), check_vma=False
    )
```

profile of v0, /device:TPU:0, one launch (start us, length us, event | category | flops | bytes accessed | tf_op | source)
XLA Modules:
  0.0 193.1 jit_solution(6788690800928492669)
XLA Ops:
  0.0 0.5 collective-permute-start.8
  0.5 2.6 %collective-permute-start = (bf16[384,512]{1,0:T(8,128)(2,1)}, bf16[384,512]{1,0:T(8,128)(2,1)S(1)}, u32[]{:S(2)}, u32[]{:S(2)}) collective-permute-start(bf16[384,512]{1,0:T(8,128)(2,1)} %refs_0_.1), channel_id=1, source_target_pairs={{0,4},{4,8},{8,12},{12,0},{1,5},{5,9},{9,13},{13,1},{2,6},{6,10},{... | collective-permute-start | bytes 1179656 | tf_op jit(solution)/shard_map/ppermute | solution.py:194
  3.1 1.5 collective-permute-start.1
  4.6 2.2 %collective-permute-start.4 = (bf16[384,512]{1,0:T(8,128)(2,1)}, bf16[384,512]{1,0:T(8,128)(2,1)S(1)}, u32[]{:S(2)}, u32[]{:S(2)}) collective-permute-start(bf16[384,512]{1,0:T(8,128)(2,1)} %refs_0_.1), channel_id=1, source_target_pairs={{0,12},{4,0},{8,4},{12,8},{1,13},{5,1},{9,5},{13,9},{2,14},{6,2},{... | collective-permute-start | bytes 1179656 | tf_op jit(solution)/shard_map/ppermute | solution.py:194
  7.1 1.1 copy.36
  8.2 3.6 %all-to-all-start = ((bf16[32,16,512]{2,0,1:T(8,128)(2,1)}), bf16[32,16,512]{2,0,1:T(8,128)(2,1)S(1)}, u32[]{:S(2)}, u32[]{:S(2)}) async-start(bf16[32,16,512]{2,0,1:T(8,128)(2,1)} %copy.36), calls=%async_computation | async-start | bytes 1048576 | tf_op jit(solution)/shard_map/all_to_all | solution.py:290
  11.7 13.2 %collective-permute-done.4.refs_3_ = bf16[384,512]{1,0:T(8,128)(2,1)S(1)} collective-permute-done((bf16[384,512]{1,0:T(8,128)(2,1)}, bf16[384,512]{1,0:T(8,128)(2,1)S(1)}, u32[]{:S(2)}, u32[]{:S(2)}) %collective-permute-start.4) | collective-permute-done | bytes 393248 | tf_op jit(solution)/shard_map/ppermute | solution.py:194
  25.0 1.3 collective-permute-start.7
  26.3 1.4 collective-permute-start.6
  27.8 0.7 collective-permute-start.3
  28.5 0.7 stack.43.places
  29.1 1.3 collective-permute-start.5
  30.5 9.9 %collective-permute-done.7 = bf16[384,512]{1,0:T(8,128)(2,1)S(1)} collective-permute-done((bf16[384,512]{1,0:T(8,128)(2,1)S(1)}, bf16[384,512]{1,0:T(8,128)(2,1)S(1)}, u32[]{:S(2)}, u32[]{:S(2)}) %collective-permute-start.7) | collective-permute-done | bytes 393248 | tf_op jit(solution)/shard_map/ppermute | solution.py:224
  40.3 0.7 copy-done.13
  41.1 1.0 broadcast_select_fusion.refs_2_
  42.2 6.7 %shard_map.118 = (f32[384,512]{1,0:T(8,128)}, f32[384,512]{1,0:T(8,128)}, f32[384,128]{1,0:T(8,128)}) custom-call(s32[16]{0:T(128)} %stack.43.places, bf16[384,512]{1,0:T(8,128)(2,1)} %refs_0_.1, bf16[384,512]{1,0:T(8,128)(2,1)} %copy-done.11, bf16[384,512]{1,0:T(8,128)(2,1)} %copy-done.10, bf16[384,512]{1,0:T(8,128)(2,1)} %copy-done.9, ...), custom_call_target="tpu_custom_call" | custom-call | flops 1 | bytes 1 | tf_op jit(solution)/shard_map/pallas_call | solution.py:64
  48.9 1.3 collective-permute-start.9
  50.3 0.8 broadcast_in_dim.46.refs_23_.slot
  51.1 9.0 %collective-permute-done.9.refs_3_ = bf16[384,512]{1,0:T(8,128)(2,1)S(1)} collective-permute-done((bf16[384,512]{1,0:T(8,128)(2,1)S(1)}, bf16[384,512]{1,0:T(8,128)(2,1)S(1)}, u32[]{:S(2)}, u32[]{:S(2)}) %collective-permute-start.9) | collective-permute-done | bytes 393248 | tf_op jit(solution)/shard_map/ppermute | solution.py:194
  60.2 0.8 copy-done.12
  60.9 7.2 %shard_map.119 = (f32[384,512]{1,0:T(8,128)}, f32[384,512]{1,0:T(8,128)}, f32[192,128]{1,0:T(8,128)}) custom-call(s32[16]{0:T(128)} %stack.43.places, bf16[384,512]{1,0:T(8,128)(2,1)} %collective-permute-done.3.refs_0_, bf16[384,512]{1,0:T(8,128)(2,1)} %collective-permute-done.5.refs_1_, bf16[384,512]{1,0:T(8,128)(2,1)} %copy-done.5, ...), custom_call_target="tpu_custom_call" | custom-call | flops 1 | bytes 1 | tf_op jit(solution)/shard_map/pallas_call | solution.py:64
  68.2 1.6 collective-permute-start.13
  69.9 1.3 collective-permute-done.10
  71.2 0.9 add_convert_fusion.4
  72.2 0.9 collective-permute-start.11
  73.0 3.3 %collective-permute-done.11 = bf16[192,128]{1,0:T(8,128)(2,1)S(1)} collective-permute-done((bf16[192,128]{1,0:T(8,128)(2,1)S(1)}, bf16[192,128]{1,0:T(8,128)(2,1)S(1)}, u32[]{:S(2)}, u32[]{:S(2)}) %collective-permute-start.11) | collective-permute-done | bytes 49184 | tf_op jit(solution)/shard_map/ppermute | solution.py:194
  76.3 6.2 %collective-permute-done.13.up_other = bf16[512,512]{1,0:T(8,128)(2,1)S(1)} collective-permute-done((bf16[512,512]{1,0:T(8,128)(2,1)S(1)}, bf16[512,512]{1,0:T(8,128)(2,1)S(1)}, u32[]{:S(2)}, u32[]{:S(2)}) %collective-permute-start.13) | collective-permute-done | bytes 524320 | tf_op jit(solution)/shard_map/ppermute | solution.py:294
  82.5 3.5 %collective-permute-start.14 = (bf16[192,128]{1,0:T(8,128)(2,1)S(1)}, bf16[192,128]{1,0:T(8,128)(2,1)S(1)}, u32[]{:S(2)}, u32[]{:S(2)}) collective-permute-start(bf16[192,128]{1,0:T(8,128)(2,1)S(1)} %add.217), channel_id=1, source_target_pairs={{0,4},{4,8},{8,12},{12,0},{1,5},{5,9},{9,13},{13,1},{2,6},{6,10},{... | collective-permute-start | bytes 147464 | tf_op jit(solution)/shard_map/ppermute | solution.py:194
  86.0 2.4 %collective-permute-start.16 = (bf16[192,128]{1,0:T(8,128)(2,1)S(1)}, bf16[192,128]{1,0:T(8,128)(2,1)S(1)}, u32[]{:S(2)}, u32[]{:S(2)}) collective-permute-start(bf16[192,128]{1,0:T(8,128)(2,1)S(1)} %add.217), channel_id=1, source_target_pairs={{0,12},{4,0},{8,4},{12,8},{1,13},{5,1},{9,5},{13,9},{2,14},{6,2},{... | collective-permute-start | bytes 147464 | tf_op jit(solution)/shard_map/ppermute | solution.py:194
  88.5 2.8 %collective-permute-done.15 = bf16[192,128]{1,0:T(8,128)(2,1)S(1)} collective-permute-done((bf16[192,128]{1,0:T(8,128)(2,1)S(1)}, bf16[192,128]{1,0:T(8,128)(2,1)S(1)}, u32[]{:S(2)}, u32[]{:S(2)}) %collective-permute-start.15) | collective-permute-done | bytes 49184 | tf_op jit(solution)/shard_map/ppermute | solution.py:194
  91.3 0.6 add_add_fusion.low
  92.0 3.6 %shard_map.120 = bf16[384,512]{1,0:T(8,128)(2,1)} custom-call(s32[1]{0:T(128)} %bitcast.8.half, f32[384,512]{1,0:T(8,128)} %get-tuple-element.42.own, f32[384,512]{1,0:T(8,128)} %copy-done.7, bf16[192,128]{1,0:T(8,128)(2,1)} %add_add_fusion.low, s32[384,1]{1,0:T(8,128)} %broadcast_in_dim.46.refs_23_.slot, bf16[512,512]{1,0:T(8,128)(2,1)} %bitcast.52, ...), custom_call_target="tpu_custom_call" | custom-call | flops 1 | bytes 1 | tf_op jit(solution)/shard_map/pallas_call | solution.py:115
  95.6 5.5 %all-to-all-start.1 = ((bf16[16,24,512]{2,1,0:T(8,128)(2,1)}), bf16[16,24,512]{2,1,0:T(8,128)(2,1)S(1)}, u32[]{:S(2)}, u32[]{:S(2)}) async-start(bf16[16,24,512]{2,1,0:T(8,128)(2,1)} %bitcast.55), calls=%async_computation.1 | async-start | bytes 786432 | tf_op jit(solution)/shard_map/all_to_all | solution.py:307
  101.2 12.0 %all-to-all-done.1 = bf16[16,24,512]{2,1,0:T(8,128)(2,1)S(1)} async-done(((bf16[16,24,512]{2,1,0:T(8,128)(2,1)}), bf16[16,24,512]{2,1,0:T(8,128)(2,1)S(1)}, u32[]{:S(2)}, u32[]{:S(2)}) %all-to-all-start.1) | async-done | bytes 393248 | tf_op jit(solution)/shard_map/all_to_all | solution.py:307
  113.4 0.2 reshape.48
  113.6 0.3 fusion.10
  114.0 5.5 %fusion.15 = (f32[8,24,8]{2,1,0:T(8,128)S(1)}, f32[8,24,8,128]{3,2,1,0:T(8,128)S(1)}) fusion(bf16[8,24,128,128]{3,2,1,0:T(8,128)(2,1)} %param.19, bf16[24,8,8,128]{3,2,1,0:T(8,128)(2,1)S(1)} %reshape.48, pred[24,128]{1,0:T(8,128)(4,1)S(1)} %iota_compare_fusion.1), kind=kOutput, calls=%fused_computation.30 | convolution fusion | flops 50723328 | bytes 7480320 | tf_op jit(solution)/shard_map/rkge,krje->krgj/dot_general | solution.py:178
  119.5 0.5 fusion.8
  120.1 4.6 %fusion.5 = bf16[24,8,8,128]{3,2,1,0:T(8,128)(2,1)S(1)} fusion(bf16[8,24,128,128]{3,2,1,0:T(8,128)(2,1)} %param.20, f32[24,8,128]{2,1,0:T(8,128)S(1)} %bitcast.58, f32[24,8,8]{2,1,0:T(8,128)S(1)} %copy.43, f32[8,24,8,128]{3,2,1,0:T(8,128)S(1)} %get-tuple-element.64, f32[8,24,8]{2,1,0:T(8,128)S(1)} %get-tuple-element.62, f32[8,24,8]{2,1,0:T(8,128)S(1)} %max.3, ...), kind=kOutput, calls=%fused_computation.4 | convolution fusion | flops 51707904 | bytes 7590912 | tf_op jit(solution)/shard_map/krgj,krje->rkge/dot_general | solution.py:187
  124.7 0.2 reshape_reshape.3
  125.2 15.5 %all_to_all.40 = bf16[16,24,512]{2,1,0:T(8,128)(2,1)S(1)} all-to-all(bf16[16,24,512]{2,1,0:T(8,128)(2,1)S(1)} %bitcast.54), channel_id=1, replica_groups=mesh['rep'=2,'z'=4,'y'=2,'core'=2] {'z','y','core'}, dimensions={0} | all-to-all | bytes 786432 | tf_op jit(solution)/shard_map/all_to_all | solution.py:313
  140.8 1.6 collective-permute-done.17.refs_1_
  142.5 0.8 copy-done.6
  143.2 3.4 %shard_map.122 = bf16[384,512]{1,0:T(8,128)(2,1)} custom-call(s32[16]{0:T(128)} %stack.43.places, bf16[384,512]{1,0:T(8,128)(2,1)} %bitcast.47, bf16[384,512]{1,0:T(8,128)(2,1)} %copy-done.6, bf16[512,8192]{1,0:T(8,128)(2,1)} %refs_2_.3, bf16[512,8192]{1,0:T(8,128)(2,1)} %collective-permute-done.18.refs_9_.refs_10_.refs_11_.refs_12_.refs_13_.refs_14_.refs_15_.refs_3_), custom_call_target="tpu_custom_call" | custom-call | flops 1 | bytes 1 | tf_op jit(solution)/shard_map/pallas_call | solution.py:156
  146.7 0.6 collective-permute-start.21
  147.3 7.5 %shard_map.121 = (bf16[384,512]{1,0:T(8,128)(2,1)}, bf16[384,512]{1,0:T(8,128)(2,1)}, bf16[384,512]{1,0:T(8,128)(2,1)}, bf16[384,512]{1,0:T(8,128)(2,1)}, bf16[3...) custom-call(s32[16]{0:T(128)} %stack.43.places, bf16[384,512]{1,0:T(8,128)(2,1)} %bitcast.48, ...), custom_call_target="tpu_custom_call" | custom-call | flops 1 | bytes 1 | tf_op jit(solution)/shard_map/pallas_call | solution.py:156
  154.7 1.5 collective-permute-start.20
  156.2 2.1 %collective-permute-done.21 = bf16[384,512]{1,0:T(8,128)(2,1)S(1)} collective-permute-done((bf16[384,512]{1,0:T(8,128)(2,1)}, bf16[384,512]{1,0:T(8,128)(2,1)S(1)}, u32[]{:S(2)}, u32[]{:S(2)}) %collective-permute-start.21) | collective-permute-done | bytes 393248 | tf_op jit(solution)/shard_map/ppermute | solution.py:194
  158.3 1.1 add_convert_fusion.3
  159.4 3.1 %collective-permute-start.22 = (bf16[384,512]{1,0:T(8,128)(2,1)S(1)}, bf16[384,512]{1,0:T(8,128)(2,1)S(1)}, u32[]{:S(2)}, u32[]{:S(2)}) collective-permute-start(bf16[384,512]{1,0:T(8,128)(2,1)S(1)} %add_convert_fusion.3), channel_id=1, source_target_pairs={{0,4},{4,8},{1,5},{5,9},{2,6},{6,10},{3,7},{7,11},{16,20},{20,24},... | collective-permute-start | bytes 1179656 | tf_op jit(solution)/shard_map/ppermute | solution.py:238
  162.5 0.6 collective-permute-start.24
  163.1 0.7 collective-permute-start.25
  163.8 1.5 collective-permute-start.19
  165.3 1.7 collective-permute-done.20
  167.0 3.3 %collective-permute-done.22 = bf16[384,512]{1,0:T(8,128)(2,1)S(1)} collective-permute-done((bf16[384,512]{1,0:T(8,128)(2,1)S(1)}, bf16[384,512]{1,0:T(8,128)(2,1)S(1)}, u32[]{:S(2)}, u32[]{:S(2)}) %collective-permute-start.22) | collective-permute-done | bytes 393248 | tf_op jit(solution)/shard_map/ppermute | solution.py:238
  170.3 1.1 add_convert_fusion.2
  171.4 2.5 %collective-permute-start.23 = (bf16[384,512]{1,0:T(8,128)(2,1)S(1)}, bf16[384,512]{1,0:T(8,128)(2,1)S(1)}, u32[]{:S(2)}, u32[]{:S(2)}) collective-permute-start(bf16[384,512]{1,0:T(8,128)(2,1)S(1)} %add_convert_fusion.2), channel_id=1, source_target_pairs={{0,4},{4,8},{8,12},{12,0},{1,5},{5,9},{9,13},{13,1},{2,6},{6,10},{... | collective-permute-start | bytes 1179656 | tf_op jit(solution)/shard_map/ppermute | solution.py:194
  174.0 1.5 collective-permute-done.24
  175.4 1.1 add_convert_fusion.1
  176.6 2.2 %collective-permute-start.26 = (bf16[384,512]{1,0:T(8,128)(2,1)S(1)}, bf16[384,512]{1,0:T(8,128)(2,1)S(1)}, u32[]{:S(2)}, u32[]{:S(2)}) collective-permute-start(bf16[384,512]{1,0:T(8,128)(2,1)S(1)} %add_convert_fusion.1), channel_id=1, source_target_pairs={{0,12},{4,0},{8,4},{12,8},{1,13},{5,1},{9,5},{13,9},{2,14},{6,2},{... | collective-permute-start | bytes 1179656 | tf_op jit(solution)/shard_map/ppermute | solution.py:194
  178.7 4.6 %collective-permute-done.19 = bf16[384,512]{1,0:T(8,128)(2,1)S(1)} collective-permute-done((bf16[384,512]{1,0:T(8,128)(2,1)}, bf16[384,512]{1,0:T(8,128)(2,1)S(1)}, u32[]{:S(2)}, u32[]{:S(2)}) %collective-permute-start.19) | collective-permute-done | bytes 393248 | tf_op jit(solution)/shard_map/ppermute | solution.py:194
  183.3 2.0 %collective-permute-done.23 = bf16[384,512]{1,0:T(8,128)(2,1)S(1)} collective-permute-done((bf16[384,512]{1,0:T(8,128)(2,1)S(1)}, bf16[384,512]{1,0:T(8,128)(2,1)S(1)}, u32[]{:S(2)}, u32[]{:S(2)}) %collective-permute-start.23) | collective-permute-done | bytes 393248 | tf_op jit(solution)/shard_map/ppermute | solution.py:194
  185.3 5.8 %collective-permute-done.26 = bf16[384,512]{1,0:T(8,128)(2,1)S(1)} collective-permute-done((bf16[384,512]{1,0:T(8,128)(2,1)S(1)}, bf16[384,512]{1,0:T(8,128)(2,1)S(1)}, u32[]{:S(2)}, u32[]{:S(2)}) %collective-permute-start.26) | collective-permute-done | bytes 393248 | tf_op jit(solution)/shard_map/ppermute | solution.py:194
  191.2 1.9 %add_convert_fusion = bf16[384,512]{1,0:T(8,128)(2,1)} fusion(bf16[384,512]{1,0:T(8,128)(2,1)S(1)} %collective-permute-done.26, bf16[384,512]{1,0:T(8,128)(2,1)S(1)} %collective-permute-done.23, bf16[384,512]{1,0:T(8,128)(2,1)S(1)} %collective-permute-done.19, bf16[384,512]{1,0:T(8,128)(2,1)} %get-tuple-element.51), kind=kLoop, calls=%fused_computation.5 | loop fusion | flops 1572864 | bytes 1966080 | tf_op jit(solution)/shard_map/convert_element_type | solution.py:336
  (68 shorter events, 1.3 us)
Async XLA Ops:
  0.0 6.9 %copy-start = (bf16[1,8192,64]{1,2,0:T(8,128)(2,1)S(1)}, bf16[1,8192,64]{1,2,0:T(8,128)(2,1)}, u32[]{:S(2)}) copy-start(bf16[1,8192,64]{1,2,0:T(8,128)(2,1)} %param.18) | copy-start | bytes 3145732
  0.0 42.2 %collective-permute-start.8 = (bf16[8192,512]{1,0:T(8,128)(2,1)}, bf16[8192,512]{1,0:T(8,128)(2,1)}, u32[]{:S(2)}, u32[]{:S(2)}) collective-permute-start(bf16[8192,512]{1,0:T(8,128)(2,1)} %refs_7_.4), channel_id=1, source_target_pairs={{0,1},{1,0},{2,3},{3,2},{4,5},{5,4},{6,7},{7,6},{8,9},{9,8},{10,11... | collective-permute-start | bytes 25165832 | tf_op jit(solution)/shard_map/ppermute | solution.py:194
  0.5 25.8 %collective-permute-start = (bf16[384,512]{1,0:T(8,128)(2,1)}, bf16[384,512]{1,0:T(8,128)(2,1)S(1)}, u32[]{:S(2)}, u32[]{:S(2)}) collective-permute-start(bf16[384,512]{1,0:T(8,128)(2,1)} %refs_0_.1), channel_id=1, source_target_pairs={{0,4},{4,8},{8,12},{12,0},{1,5},{5,9},{9,13},{13,1},{2,6},{6,10},{... | collective-permute-start | bytes 1179656 | tf_op jit(solution)/shard_map/ppermute | solution.py:194
  3.1 23.2 %collective-permute-start.1 = (bf16[384,512]{1,0:T(8,128)(2,1)}, bf16[384,512]{1,0:T(8,128)(2,1)S(1)}, u32[]{:S(2)}, u32[]{:S(2)}) collective-permute-start(bf16[384,512]{1,0:T(8,128)(2,1)} %refs_0_.1), channel_id=1, source_target_pairs={{0,2},{2,0},{1,3},{3,1},{4,6},{6,4},{5,7},{7,5},{8,10},{10,8},{9,1... | collective-permute-start | bytes 1179656 | tf_op jit(solution)/shard_map/ppermute | solution.py:194
  4.6 20.4 %collective-permute-start.4 = (bf16[384,512]{1,0:T(8,128)(2,1)}, bf16[384,512]{1,0:T(8,128)(2,1)S(1)}, u32[]{:S(2)}, u32[]{:S(2)}) collective-permute-start(bf16[384,512]{1,0:T(8,128)(2,1)} %refs_0_.1), channel_id=1, source_target_pairs={{0,12},{4,0},{8,4},{12,8},{1,13},{5,1},{9,5},{13,9},{2,14},{6,2},{... | collective-permute-start | bytes 1179656 | tf_op jit(solution)/shard_map/ppermute | solution.py:194
  6.9 19.4 %collective-permute-start.2 = (bf16[1,64,8192]{2,1,0:T(8,128)(2,1)}, bf16[1,64,8192]{2,1,0:T(8,128)(2,1)S(1)}, u32[]{:S(2)}, u32[]{:S(2)}) collective-permute-start(bf16[1,64,8192]{2,1,0:T(8,128)(2,1)} %bitcast.37), channel_id=1, source_target_pairs={{0,1},{1,0},{2,3},{3,2},{4,5},{5,4},{6,7},{7,6},{8,9},{9,8},{10,11... | collective-permute-start | bytes 3145736 | tf_op jit(solution)/shard_map/ppermute | solution.py:194
  8.2 40.8 %all-to-all-start = ((bf16[32,16,512]{2,0,1:T(8,128)(2,1)}), bf16[32,16,512]{2,0,1:T(8,128)(2,1)S(1)}, u32[]{:S(2)}, u32[]{:S(2)}) async-start(bf16[32,16,512]{2,0,1:T(8,128)(2,1)} %copy.36), calls=%async_computation | async-start | bytes 1048576 | tf_op jit(solution)/shard_map/all_to_all | solution.py:290
  25.0 17.2 %copy-start.9 = (bf16[384,512]{1,0:T(8,128)(2,1)}, bf16[384,512]{1,0:T(8,128)(2,1)S(1)}, u32[]{:S(2)}) copy-start(bf16[384,512]{1,0:T(8,128)(2,1)S(1)} %collective-permute-done.4.refs_3_) | copy-start | bytes 1179652
  25.0 15.4 %collective-permute-start.7 = (bf16[384,512]{1,0:T(8,128)(2,1)S(1)}, bf16[384,512]{1,0:T(8,128)(2,1)S(1)}, u32[]{:S(2)}, u32[]{:S(2)}) collective-permute-start(bf16[384,512]{1,0:T(8,128)(2,1)S(1)} %collective-permute-done.4.refs_3_), channel_id=1, source_target_pairs={{8,4},{4,0},{9,5},{5,1},{10,6},{6,2},{11,7},{7,3},{24,20},{20,16},... | collective-permute-start | bytes 1179656 | tf_op jit(solution)/shard_map/ppermute | solution.py:224
  26.3 15.9 %copy-start.10 = (bf16[384,512]{1,0:T(8,128)(2,1)}, bf16[384,512]{1,0:T(8,128)(2,1)S(1)}, u32[]{:S(2)}) copy-start(bf16[384,512]{1,0:T(8,128)(2,1)S(1)} %collective-permute-done.refs_2_) | copy-start | bytes 1179652
  26.3 15.9 %copy-start.11 = (bf16[384,512]{1,0:T(8,128)(2,1)}, bf16[384,512]{1,0:T(8,128)(2,1)S(1)}, u32[]{:S(2)}) copy-start(bf16[384,512]{1,0:T(8,128)(2,1)S(1)} %collective-permute-done.1.refs_1_) | copy-start | bytes 1179652
  26.3 15.9 %copy-start.2 = (bf16[1,64,8192]{2,1,0:T(8,128)(2,1)}, bf16[1,64,8192]{2,1,0:T(8,128)(2,1)S(1)}, u32[]{:S(2)}) copy-start(bf16[1,64,8192]{2,1,0:T(8,128)(2,1)S(1)} %collective-permute-done.2.refs_16_.refs_17_.refs_18_.refs_19_) | copy-start | bytes 3145732
  26.3 14.8 %collective-permute-start.6 = (bf16[384,512]{1,0:T(8,128)(2,1)S(1)}, bf16[384,512]{1,0:T(8,128)(2,1)}, u32[]{:S(2)}, u32[]{:S(2)}) collective-permute-start(bf16[384,512]{1,0:T(8,128)(2,1)S(1)} %collective-permute-done.refs_2_), channel_id=1, source_target_pairs={{4,8},{8,12},{5,9},{9,13},{6,10},{10,14},{7,11},{11,15},{20,24},{2... | collective-permute-start | bytes 1179656 | tf_op jit(solution)/shard_map/ppermute | solution.py:222
  27.8 21.2 %collective-permute-start.3 = (bf16[384,512]{1,0:T(8,128)(2,1)S(1)}, bf16[384,512]{1,0:T(8,128)(2,1)}, u32[]{:S(2)}, u32[]{:S(2)}) collective-permute-start(bf16[384,512]{1,0:T(8,128)(2,1)S(1)} %collective-permute-done.refs_2_), channel_id=1, source_target_pairs={{0,2},{2,0},{1,3},{3,1},{4,6},{6,4},{5,7},{7,5},{8,10},{10,8},{9,1... | collective-permute-start | bytes 1179656 | tf_op jit(solution)/shard_map/ppermute | solution.py:194
  29.1 22.0 %collective-permute-start.5 = (bf16[384,512]{1,0:T(8,128)(2,1)S(1)}, bf16[384,512]{1,0:T(8,128)(2,1)}, u32[]{:S(2)}, u32[]{:S(2)}) collective-permute-start(bf16[384,512]{1,0:T(8,128)(2,1)S(1)} %collective-permute-done.4.refs_3_), channel_id=1, source_target_pairs={{0,2},{2,0},{1,3},{3,1},{4,6},{6,4},{5,7},{7,5},{8,10},{10,8},{9,1... | collective-permute-start | bytes 1179656 | tf_op jit(solution)/shard_map/ppermute | solution.py:194
  40.3 0.7 copy-start.13
  42.1 6.8 %copy-start.5 = (bf16[384,512]{1,0:T(8,128)(2,1)}, bf16[384,512]{1,0:T(8,128)(2,1)S(1)}, u32[]{:S(2)}) copy-start(bf16[384,512]{1,0:T(8,128)(2,1)S(1)} %broadcast_select_fusion.refs_2_) | copy-start | bytes 1179652
  42.1 8.1 %copy-start.16 = (s32[384,1]{0,1:T(1,128)S(1)}, s32[384,1]{0,1:T(1,128)}, u32[]{:S(2)}) copy-start(s32[384,1]{0,1:T(1,128)} %param.13) | copy-start | bytes 4612
  42.1 8.1 %copy-start.17 = (s32[16]{0:T(128)S(1)}, s32[16]{0:T(128)}, u32[]{:S(2)}) copy-start(s32[16]{0:T(128)} %param.14) | copy-start | bytes 196
  48.9 19.3 %copy-start.4 = (bf16[32,16,512]{2,0,1:T(8,128)(2,1)}, bf16[32,16,512]{2,0,1:T(8,128)(2,1)S(1)}, u32[]{:S(2)}) copy-start(bf16[32,16,512]{2,0,1:T(8,128)(2,1)S(1)} %all-to-all-done) | copy-start | bytes 1572868
  48.9 11.2 %collective-permute-start.9 = (bf16[384,512]{1,0:T(8,128)(2,1)S(1)}, bf16[384,512]{1,0:T(8,128)(2,1)S(1)}, u32[]{:S(2)}, u32[]{:S(2)}) collective-permute-start(bf16[384,512]{1,0:T(8,128)(2,1)S(1)} %broadcast_select_fusion.refs_2_), channel_id=1, source_target_pairs={{0,2},{2,0},{1,3},{3,1},{4,6},{6,4},{5,7},{7,5},{8,10},{10,8},{9,1... | collective-permute-start | bytes 1179656 | tf_op jit(solution)/shard_map/ppermute | solution.py:194
  51.1 49.9 %copy-start.14 = (bf16[24,1024]{1,0:T(8,128)(2,1)S(1)}, bf16[24,1024]{1,0:T(8,128)(2,1)}, u32[]{:S(2)}) copy-start(bf16[24,1024]{1,0:T(8,128)(2,1)} %param.21) | copy-start | bytes 147460
  51.1 50.0 %copy-start.15 = (bf16[24,1024]{1,0:T(8,128)(2,1)S(1)}, bf16[24,1024]{1,0:T(8,128)(2,1)}, u32[]{:S(2)}) copy-start(bf16[24,1024]{1,0:T(8,128)(2,1)} %param.22) | copy-start | bytes 147460
  51.1 50.0 %copy-start.18 = (s32[24]{0:T(128)S(1)}, s32[24]{0:T(128)}, u32[]{:S(2)}) copy-start(s32[24]{0:T(128)} %param.15) | copy-start | bytes 292
  60.2 0.8 copy-start.12
  68.2 14.4 %collective-permute-start.12 = (f32[384,512]{1,0:T(8,128)}, f32[384,512]{1,0:T(8,128)S(1)}, u32[]{:S(2)}, u32[]{:S(2)}) collective-permute-start(f32[384,512]{1,0:T(8,128)} %get-tuple-element.44), channel_id=1, source_target_pairs={{0,1},{1,0},{2,3},{3,2},{4,5},{5,4},{6,7},{7,6},{8,9},{9,8},{10,11... | collective-permute-start | bytes 2359304 | tf_op jit(solution)/shard_map/ppermute | solution.py:194
  68.2 14.3 %collective-permute-start.13 = (bf16[512,512]{1,0:T(8,128)(2,1)S(1)}, bf16[512,512]{1,0:T(8,128)(2,1)S(1)}, u32[]{:S(2)}, u32[]{:S(2)}) collective-permute-start(bf16[512,512]{1,0:T(8,128)(2,1)S(1)} %bitcast.51), channel_id=1, source_target_pairs={{0,16},{16,0},{1,17},{17,1},{2,18},{18,2},{3,19},{19,3},{4,20},{20... | collective-permute-start | bytes 1572872 | tf_op jit(solution)/shard_map/ppermute | solution.py:294
  69.7 1.5 collective-permute-start.10
  72.2 4.2 %collective-permute-start.11 = (bf16[192,128]{1,0:T(8,128)(2,1)S(1)}, bf16[192,128]{1,0:T(8,128)(2,1)S(1)}, u32[]{:S(2)}, u32[]{:S(2)}) collective-permute-start(bf16[192,128]{1,0:T(8,128)(2,1)S(1)} %add_convert_fusion.4), channel_id=1, source_target_pairs={{0,2},{2,0},{1,3},{3,1},{4,6},{6,4},{5,7},{7,5},{8,10},{10,8},{9,1... | collective-permute-start | bytes 147464 | tf_op jit(solution)/shard_map/ppermute | solution.py:194
  82.5 9.5 %copy-start.8 = (bf16[512,512]{1,0:T(8,128)(2,1)}, bf16[512,512]{1,0:T(8,128)(2,1)S(1)}, u32[]{:S(2)}) copy-start(bf16[512,512]{1,0:T(8,128)(2,1)S(1)} %collective-permute-done.13.up_other) | copy-start | bytes 1572868
  82.5 9.5 %copy-start.7 = (f32[384,512]{1,0:T(8,128)}, f32[384,512]{1,0:T(8,128)S(1)}, u32[]{:S(2)}) copy-start(f32[384,512]{1,0:T(8,128)S(1)} %collective-permute-done.12.received) | copy-start | bytes 2359300
  82.5 6.0 %collective-permute-start.14 = (bf16[192,128]{1,0:T(8,128)(2,1)S(1)}, bf16[192,128]{1,0:T(8,128)(2,1)S(1)}, u32[]{:S(2)}, u32[]{:S(2)}) collective-permute-start(bf16[192,128]{1,0:T(8,128)(2,1)S(1)} %add.217), channel_id=1, source_target_pairs={{0,4},{4,8},{8,12},{12,0},{1,5},{5,9},{9,13},{13,1},{2,6},{6,10},{... | collective-permute-start | bytes 147464 | tf_op jit(solution)/shard_map/ppermute | solution.py:194
  86.0 5.3 %collective-permute-start.15 = (bf16[192,128]{1,0:T(8,128)(2,1)S(1)}, bf16[192,128]{1,0:T(8,128)(2,1)S(1)}, u32[]{:S(2)}, u32[]{:S(2)}) collective-permute-start(bf16[192,128]{1,0:T(8,128)(2,1)S(1)} %add.217), channel_id=1, source_target_pairs={{0,8},{4,12},{8,0},{12,4},{1,9},{5,13},{9,1},{13,5},{2,10},{6,14},... | collective-permute-start | bytes 147464 | tf_op jit(solution)/shard_map/ppermute | solution.py:194
  86.0 5.3 %collective-permute-start.16 = (bf16[192,128]{1,0:T(8,128)(2,1)S(1)}, bf16[192,128]{1,0:T(8,128)(2,1)S(1)}, u32[]{:S(2)}, u32[]{:S(2)}) collective-permute-start(bf16[192,128]{1,0:T(8,128)(2,1)S(1)} %add.217), channel_id=1, source_target_pairs={{0,12},{4,0},{8,4},{12,8},{1,13},{5,1},{9,5},{13,9},{2,14},{6,2},{... | collective-permute-start | bytes 147464 | tf_op jit(solution)/shard_map/ppermute | solution.py:194
  95.6 46.9 %collective-permute-start.18 = (bf16[512,8192]{1,0:T(8,128)(2,1)}, bf16[512,8192]{1,0:T(8,128)(2,1)}, u32[]{:S(2)}, u32[]{:S(2)}) collective-permute-start(bf16[512,8192]{1,0:T(8,128)(2,1)} %refs_2_.3), channel_id=1, source_target_pairs={{0,1},{1,0},{2,3},{3,2},{4,5},{5,4},{6,7},{7,6},{8,9},{9,8},{10,11... | collective-permute-start | bytes 25165832 | tf_op jit(solution)/shard_map/ppermute | solution.py:194
  95.6 17.7 %all-to-all-start.1 = ((bf16[16,24,512]{2,1,0:T(8,128)(2,1)}), bf16[16,24,512]{2,1,0:T(8,128)(2,1)S(1)}, u32[]{:S(2)}, u32[]{:S(2)}) async-start(bf16[16,24,512]{2,1,0:T(8,128)(2,1)} %bitcast.55), calls=%async_computation.1 | async-start | bytes 786432 | tf_op jit(solution)/shard_map/all_to_all | solution.py:307
  140.7 1.7 copy-start.3
  140.7 1.7 collective-permute-start.17
  142.5 0.8 copy-start.6
  146.7 11.7 %collective-permute-start.21 = (bf16[384,512]{1,0:T(8,128)(2,1)}, bf16[384,512]{1,0:T(8,128)(2,1)S(1)}, u32[]{:S(2)}, u32[]{:S(2)}) collective-permute-start(bf16[384,512]{1,0:T(8,128)(2,1)} %shard_map.122), channel_id=1, source_target_pairs={{0,2},{2,0},{1,3},{3,1},{4,6},{6,4},{5,7},{7,5},{8,10},{10,8},{9,1... | collective-permute-start | bytes 1179656 | tf_op jit(solution)/shard_map/ppermute | solution.py:194
  147.3 45.8 %copy-start.1 = (bf16[1,8192,64]{1,2,0:T(8,128)(2,1)S(1)}, bf16[1,8192,64]{1,2,0:T(8,128)(2,1)}, u32[]{:S(2)}) copy-start(bf16[1,8192,64]{1,2,0:T(8,128)(2,1)} %param.18) | copy-start | bytes 3145732
  154.7 12.2 %collective-permute-start.20 = (bf16[384,512]{1,0:T(8,128)(2,1)}, bf16[384,512]{1,0:T(8,128)(2,1)S(1)}, u32[]{:S(2)}, u32[]{:S(2)}) collective-permute-start(bf16[384,512]{1,0:T(8,128)(2,1)} %get-tuple-element.55), channel_id=1, source_target_pairs={{0,2},{2,0},{1,3},{3,1},{4,6},{6,4},{5,7},{7,5},{8,10},{10,8},{9,1... | collective-permute-start | bytes 1179656 | tf_op jit(solution)/shard_map/ppermute | solution.py:194
  159.4 10.8 %collective-permute-start.22 = (bf16[384,512]{1,0:T(8,128)(2,1)S(1)}, bf16[384,512]{1,0:T(8,128)(2,1)S(1)}, u32[]{:S(2)}, u32[]{:S(2)}) collective-permute-start(bf16[384,512]{1,0:T(8,128)(2,1)S(1)} %add_convert_fusion.3), channel_id=1, source_target_pairs={{0,4},{4,8},{1,5},{5,9},{2,6},{6,10},{3,7},{7,11},{16,20},{20,24},... | collective-permute-start | bytes 1179656 | tf_op jit(solution)/shard_map/ppermute | solution.py:238
  162.5 12.9 %collective-permute-start.24 = (bf16[384,512]{1,0:T(8,128)(2,1)}, bf16[384,512]{1,0:T(8,128)(2,1)S(1)}, u32[]{:S(2)}, u32[]{:S(2)}) collective-permute-start(bf16[384,512]{1,0:T(8,128)(2,1)} %get-tuple-element.60), channel_id=1, source_target_pairs={{0,2},{2,0},{1,3},{3,1},{4,6},{6,4},{5,7},{7,5},{8,10},{10,8},{9,1... | collective-permute-start | bytes 1179656 | tf_op jit(solution)/shard_map/ppermute | solution.py:194
  163.1 12.3 %collective-permute-start.25 = (bf16[384,512]{1,0:T(8,128)(2,1)S(1)}, bf16[384,512]{1,0:T(8,128)(2,1)S(1)}, u32[]{:S(2)}, u32[]{:S(2)}) collective-permute-start(bf16[384,512]{1,0:T(8,128)(2,1)S(1)} %add_convert_fusion.3), channel_id=1, source_target_pairs={{12,8},{8,4},{13,9},{9,5},{14,10},{10,6},{15,11},{11,7},{28,24},{2... | collective-permute-start | bytes 1179656 | tf_op jit(solution)/shard_map/ppermute | solution.py:239
  163.8 19.5 %collective-permute-start.19 = (bf16[384,512]{1,0:T(8,128)(2,1)}, bf16[384,512]{1,0:T(8,128)(2,1)S(1)}, u32[]{:S(2)}, u32[]{:S(2)}) collective-permute-start(bf16[384,512]{1,0:T(8,128)(2,1)} %get-tuple-element.52), channel_id=1, source_target_pairs={{0,2},{2,0},{1,3},{3,1},{4,6},{6,4},{5,7},{7,5},{8,10},{10,8},{9,1... | collective-permute-start | bytes 1179656 | tf_op jit(solution)/shard_map/ppermute | solution.py:194
  171.4 13.9 %collective-permute-start.23 = (bf16[384,512]{1,0:T(8,128)(2,1)S(1)}, bf16[384,512]{1,0:T(8,128)(2,1)S(1)}, u32[]{:S(2)}, u32[]{:S(2)}) collective-permute-start(bf16[384,512]{1,0:T(8,128)(2,1)S(1)} %add_convert_fusion.2), channel_id=1, source_target_pairs={{0,4},{4,8},{8,12},{12,0},{1,5},{5,9},{9,13},{13,1},{2,6},{6,10},{... | collective-permute-start | bytes 1179656 | tf_op jit(solution)/shard_map/ppermute | solution.py:194
  176.6 14.6 %collective-permute-start.26 = (bf16[384,512]{1,0:T(8,128)(2,1)S(1)}, bf16[384,512]{1,0:T(8,128)(2,1)S(1)}, u32[]{:S(2)}, u32[]{:S(2)}) collective-permute-start(bf16[384,512]{1,0:T(8,128)(2,1)S(1)} %add_convert_fusion.1), channel_id=1, source_target_pairs={{0,12},{4,0},{8,4},{12,8},{1,13},{5,1},{9,5},{13,9},{2,14},{6,2},{... | collective-permute-start | bytes 1179656 | tf_op jit(solution)/shard_map/ppermute | solution.py:194
where the time goes:
time: 194 us; the launch traced here: 193 us
  waiting for transfers between devices  80.4 us (41%)
  starting transfers between devices  43.2 us (22%)
  Pallas kernels  28.4 us (15%)
  blocking collectives  15.5 us (8%)
  matrix products  10.4 us (5%)
  other arithmetic  8.73 us (4%)
  local copies, waits for them, and re-layouts  6 us (3%)
    ppermute x22, waiting for transfers between devices, shift(): lax.ppermute(value, axis, [(i, (i + by) % size) for i in range(size)])  49 us
    ppermute x22, starting transfers between devices, shift(): lax.ppermute(value, axis, [(i, (i + by) % size) for i in range(size)])  26.2 us
    all_to_all x1, blocking collectives, shards(): lax.all_to_all(context, ADP, split_axis=0, concat_axis=0, tiled=True)  15.5 us
    pallas_call x2, Pallas kernels, project(): pl.pallas_call(kernel, grid_spec=pltpu.PrefetchScalarGridSpec(num_scalar_...  13.9 us
    all_to_all x1, waiting for transfers between devices, shards(): lax.all_to_all(query, ADP, split_axis=0, concat_axis=1, tiled=True)  12 us
    pallas_call x2, Pallas kernels, output_partial(): pl.pallas_call(kernel, grid_spec=pltpu.PrefetchScalarGridSpec(num_scalar_...  10.9 us
    ppermute x1, waiting for transfers between devices, gather_features(): from_above = lax.ppermute(above, 'z', [(2, 1), (1, 0)])  9.86 us
    ppermute x1, waiting for transfers between devices, shards(): lax.ppermute(up, 'rep', [(i, i ^ 1) for i in range(lax.axis_size('rep'))])  6.19 us
  transfers between devices with their start and end apart: 29, of which 16 were waited for; matrix products, arithmetic and copies ran while one was open for 10% of the time, Pallas kernels for 7%

commit v1 on v0

--- a/solution.py
+++ b/solution.py
@@ -224,7 +224,7 @@
     from_above = lax.ppermute(above, "z", [(2, 1), (1, 0)])
     sums = begin([tokens, side, below, above])
     two = jnp.where(z >= 2, from_below, from_above)
-    two, _, up, sums = lax.optimization_barrier((two, below_side, up, sums))
+    two, _, up = lax.optimization_barrier((two, below_side, up))
     return sums, [below_side, above_side, two, shift(two, "y", 1)], up
 
 
@@ -297,9 +297,10 @@
 
     low = (low + shift(low, "core", 1)).astype(jnp.bfloat16)
     received = shift(sent, "core", 1)
+    low, up_other = lax.optimization_barrier((low, up_other))
     if sides == 2:
         low = low + shift(low, "y", 1)
-    low, received, up_other = lax.optimization_barrier((low, received, up_other))
+    low, received = lax.optimization_barrier((low, received))
     low = sum([shift(low, "z", k) for k in range(1, layers)], low)
 
     query = make_query(half.astype(jnp.int32).reshape(1), own, received, low, slot, up, up_other)

time: 194 us -> 193 us (level)
    ppermute x22, waiting for transfers between devices: 49 us -> 42.8 us  [shift(): lax.ppermute(value, axis, [(i, (i + by) % size) for i in range(size)])]
    ppermute x1, waiting for transfers between devices: 6.19 us -> 10.3 us  [shards(): lax.ppermute(up, 'rep', [(i, i ^ 1) for i in range(lax.axis_size('rep'))])]
  transfers between devices with their start and end apart: 29 -> 29, of which waited for: 16 -> 17; matrix products, arithmetic and copies ran while one was open for 10% -> 11% of each run, Pallas kernels for 7% -> 7%
where the time goes in v1:
time: 193 us; the launch traced here: 192 us
  waiting for transfers between devices  79 us (41%)
  starting transfers between devices  43.2 us (22%)
  Pallas kernels  28.4 us (15%)
  blocking collectives  15.5 us (8%)
  matrix products  10.4 us (5%)
  other arithmetic  10 us (5%)
  local copies, waits for them, and re-layouts  5.12 us (3%)
    ppermute x22, waiting for transfers between devices, shift(): lax.ppermute(value, axis, [(i, (i + by) % size) for i in range(size)])  42.8 us
    ppermute x22, starting transfers between devices, shift(): lax.ppermute(value, axis, [(i, (i + by) % size) for i in range(size)])  26.2 us
    all_to_all x1, blocking collectives, shards(): lax.all_to_all(context, ADP, split_axis=0, concat_axis=0, tiled=True)  15.5 us
    pallas_call x2, Pallas kernels, project(): pl.pallas_call(kernel, grid_spec=pltpu.PrefetchScalarGridSpec(num_scalar_...  13.9 us
    all_to_all x1, waiting for transfers between devices, shards(): lax.all_to_all(query, ADP, split_axis=0, concat_axis=1, tiled=True)  12 us
    pallas_call x2, Pallas kernels, output_partial(): pl.pallas_call(kernel, grid_spec=pltpu.PrefetchScalarGridSpec(num_scalar_...  10.9 us
    ppermute x1, waiting for transfers between devices, gather_features(): from_above = lax.ppermute(above, 'z', [(2, 1), (1, 0)])  10.6 us
    ppermute x1, waiting for transfers between devices, shards(): lax.ppermute(up, 'rep', [(i, i ^ 1) for i in range(lax.axis_size('rep'))])  10.3 us
  transfers between devices with their start and end apart: 29, of which 17 were waited for; matrix products, arithmetic and copies ran while one was open for 11% of the time, Pallas kernels for 7%

profile of v1, /device:TPU:0, one launch (start us, length us, event | category | flops | bytes accessed | tf_op | source)
XLA Modules:
  0.0 192.1 jit_solution(11456918896721002077)
XLA Ops:
  0.0 0.5 collective-permute-start.9
  0.5 2.6 %collective-permute-start = (bf16[384,512]{1,0:T(8,128)(2,1)}, bf16[384,512]{1,0:T(8,128)(2,1)S(1)}, u32[]{:S(2)}, u32[]{:S(2)}) collective-permute-start(bf16[384,512]{1,0:T(8,128)(2,1)} %refs_0_.1), channel_id=1, source_target_pairs={{0,4},{4,8},{8,12},{12,0},{1,5},{5,9},{9,13},{13,1},{2,6},{6,10},{... | collective-permute-start | bytes 1179656 | tf_op jit(solution)/shard_map/ppermute | solution.py:194
  3.1 1.5 collective-permute-start.1
  4.6 2.2 %collective-permute-start.4 = (bf16[384,512]{1,0:T(8,128)(2,1)}, bf16[384,512]{1,0:T(8,128)(2,1)S(1)}, u32[]{:S(2)}, u32[]{:S(2)}) collective-permute-start(bf16[384,512]{1,0:T(8,128)(2,1)} %refs_0_.1), channel_id=1, source_target_pairs={{0,12},{4,0},{8,4},{12,8},{1,13},{5,1},{9,5},{13,9},{2,14},{6,2},{... | collective-permute-start | bytes 1179656 | tf_op jit(solution)/shard_map/ppermute | solution.py:194
  7.1 1.1 copy.36
  8.2 3.6 %all-to-all-start = ((bf16[32,16,512]{2,0,1:T(8,128)(2,1)}), bf16[32,16,512]{2,0,1:T(8,128)(2,1)S(1)}, u32[]{:S(2)}, u32[]{:S(2)}) async-start(bf16[32,16,512]{2,0,1:T(8,128)(2,1)} %copy.36), calls=%async_computation | async-start | bytes 1048576 | tf_op jit(solution)/shard_map/all_to_all | solution.py:290
  11.7 13.2 %collective-permute-done.4.refs_3_ = bf16[384,512]{1,0:T(8,128)(2,1)S(1)} collective-permute-done((bf16[384,512]{1,0:T(8,128)(2,1)}, bf16[384,512]{1,0:T(8,128)(2,1)S(1)}, u32[]{:S(2)}, u32[]{:S(2)}) %collective-permute-start.4) | collective-permute-done | bytes 393248 | tf_op jit(solution)/shard_map/ppermute | solution.py:194
  25.0 1.3 collective-permute-start.7
  26.3 1.4 collective-permute-start.6
  27.7 0.7 collective-permute-start.3
  28.4 1.3 collective-permute-start.5
  29.8 10.6 %collective-permute-done.7 = bf16[384,512]{1,0:T(8,128)(2,1)S(1)} collective-permute-done((bf16[384,512]{1,0:T(8,128)(2,1)S(1)}, bf16[384,512]{1,0:T(8,128)(2,1)S(1)}, u32[]{:S(2)}, u32[]{:S(2)}) %collective-permute-start.7) | collective-permute-done | bytes 393248 | tf_op jit(solution)/shard_map/ppermute | solution.py:224
  40.3 0.7 copy-done.12
  41.1 1.0 broadcast_select_fusion.refs_2_
  42.2 1.2 collective-permute-start.8
  43.4 0.7 reduce
  44.1 0.7 select_reduce_fusion
  44.9 0.8 broadcast_in_dim.46.refs_23_.slot
  45.7 0.6 stack.43.places
  46.3 6.6 %shard_map.118 = (f32[384,512]{1,0:T(8,128)}, f32[384,512]{1,0:T(8,128)}, f32[384,128]{1,0:T(8,128)}) custom-call(s32[16]{0:T(128)} %stack.43.places, bf16[384,512]{1,0:T(8,128)(2,1)} %refs_0_.1, bf16[384,512]{1,0:T(8,128)(2,1)} %copy-done.10, bf16[384,512]{1,0:T(8,128)(2,1)} %copy-done.9, bf16[384,512]{1,0:T(8,128)(2,1)} %copy-done.11, ...), custom_call_target="tpu_custom_call" | custom-call | flops 1 | bytes 1 | tf_op jit(solution)/shard_map/pallas_call | solution.py:64
  52.9 3.3 %collective-permute-done.8.refs_3_ = bf16[384,512]{1,0:T(8,128)(2,1)} collective-permute-done((bf16[384,512]{1,0:T(8,128)(2,1)S(1)}, bf16[384,512]{1,0:T(8,128)(2,1)}, u32[]{:S(2)}, u32[]{:S(2)}) %collective-permute-start.8) | collective-permute-done | bytes 393248 | tf_op jit(solution)/shard_map/ppermute | solution.py:194
  56.2 7.3 %shard_map.119 = (f32[384,512]{1,0:T(8,128)}, f32[384,512]{1,0:T(8,128)}, f32[192,128]{1,0:T(8,128)}) custom-call(s32[16]{0:T(128)} %stack.43.places, bf16[384,512]{1,0:T(8,128)(2,1)} %collective-permute-done.3.refs_0_, bf16[384,512]{1,0:T(8,128)(2,1)} %collective-permute-done.5.refs_1_, bf16[384,512]{1,0:T(8,128)(2,1)} %copy-done.5, ...), custom_call_target="tpu_custom_call" | custom-call | flops 1 | bytes 1 | tf_op jit(solution)/shard_map/pallas_call | solution.py:64
  63.5 1.6 collective-permute-start.11
  65.3 1.3 collective-permute-done.10
  66.7 0.9 add_convert_fusion.4
  67.6 10.3 %collective-permute-done.11.up_other = bf16[512,512]{1,0:T(8,128)(2,1)S(1)} collective-permute-done((bf16[512,512]{1,0:T(8,128)(2,1)S(1)}, bf16[512,512]{1,0:T(8,128)(2,1)S(1)}, u32[]{:S(2)}, u32[]{:S(2)}) %collective-permute-start.11) | collective-permute-done | bytes 524320 | tf_op jit(solution)/shard_map/ppermute | solution.py:294
  77.9 1.0 collective-permute-start.12
  78.9 3.1 %collective-permute-done.12 = bf16[192,128]{1,0:T(8,128)(2,1)S(1)} collective-permute-done((bf16[192,128]{1,0:T(8,128)(2,1)S(1)}, bf16[192,128]{1,0:T(8,128)(2,1)S(1)}, u32[]{:S(2)}, u32[]{:S(2)}) %collective-permute-start.12) | collective-permute-done | bytes 49184 | tf_op jit(solution)/shard_map/ppermute | solution.py:194
  82.0 2.8 %collective-permute-start.14 = (bf16[192,128]{1,0:T(8,128)(2,1)S(1)}, bf16[192,128]{1,0:T(8,128)(2,1)S(1)}, u32[]{:S(2)}, u32[]{:S(2)}) collective-permute-start(bf16[192,128]{1,0:T(8,128)(2,1)S(1)} %add.217), channel_id=1, source_target_pairs={{0,4},{4,8},{8,12},{12,0},{1,5},{5,9},{9,13},{13,1},{2,6},{6,10},{... | collective-permute-start | bytes 147464 | tf_op jit(solution)/shard_map/ppermute | solution.py:194
  84.9 2.8 %collective-permute-start.16 = (bf16[192,128]{1,0:T(8,128)(2,1)S(1)}, bf16[192,128]{1,0:T(8,128)(2,1)S(1)}, u32[]{:S(2)}, u32[]{:S(2)}) collective-permute-start(bf16[192,128]{1,0:T(8,128)(2,1)S(1)} %add.217), channel_id=1, source_target_pairs={{0,12},{4,0},{8,4},{12,8},{1,13},{5,1},{9,5},{13,9},{2,14},{6,2},{... | collective-permute-start | bytes 147464 | tf_op jit(solution)/shard_map/ppermute | solution.py:194
  87.8 0.3 collective-permute-done.14
  88.1 2.2 %collective-permute-done.15 = bf16[192,128]{1,0:T(8,128)(2,1)S(1)} collective-permute-done((bf16[192,128]{1,0:T(8,128)(2,1)S(1)}, bf16[192,128]{1,0:T(8,128)(2,1)S(1)}, u32[]{:S(2)}, u32[]{:S(2)}) %collective-permute-start.15) | collective-permute-done | bytes 49184 | tf_op jit(solution)/shard_map/ppermute | solution.py:194
  90.4 0.6 add_add_fusion.low
  91.0 3.6 %shard_map.120 = bf16[384,512]{1,0:T(8,128)(2,1)} custom-call(s32[1]{0:T(128)} %bitcast.8.half, f32[384,512]{1,0:T(8,128)} %get-tuple-element.37.own, f32[384,512]{1,0:T(8,128)} %copy-done.7, bf16[192,128]{1,0:T(8,128)(2,1)} %add_add_fusion.low, s32[384,1]{1,0:T(8,128)} %broadcast_in_dim.46.refs_23_.slot, bf16[512,512]{1,0:T(8,128)(2,1)} %bitcast.52, ...), custom_call_target="tpu_custom_call" | custom-call | flops 1 | bytes 1 | tf_op jit(solution)/shard_map/pallas_call | solution.py:115
  94.6 5.4 %all-to-all-start.1 = ((bf16[16,24,512]{2,1,0:T(8,128)(2,1)}), bf16[16,24,512]{2,1,0:T(8,128)(2,1)S(1)}, u32[]{:S(2)}, u32[]{:S(2)}) async-start(bf16[16,24,512]{2,1,0:T(8,128)(2,1)} %bitcast.55), calls=%async_computation.1 | async-start | bytes 786432 | tf_op jit(solution)/shard_map/all_to_all | solution.py:308
  100.2 12.0 %all-to-all-done.1 = bf16[16,24,512]{2,1,0:T(8,128)(2,1)S(1)} async-done(((bf16[16,24,512]{2,1,0:T(8,128)(2,1)}), bf16[16,24,512]{2,1,0:T(8,128)(2,1)S(1)}, u32[]{:S(2)}, u32[]{:S(2)}) %all-to-all-start.1) | async-done | bytes 393248 | tf_op jit(solution)/shard_map/all_to_all | solution.py:308
  112.6 0.3 fusion.10
  112.9 5.5 %fusion.15 = (f32[8,24,8]{2,1,0:T(8,128)S(1)}, f32[8,24,8,128]{3,2,1,0:T(8,128)S(1)}) fusion(bf16[8,24,128,128]{3,2,1,0:T(8,128)(2,1)} %param.19, bf16[24,8,8,128]{3,2,1,0:T(8,128)(2,1)S(1)} %reshape.48, pred[24,128]{1,0:T(8,128)(4,1)S(1)} %iota_compare_fusion.1), kind=kOutput, calls=%fused_computation.30 | convolution fusion | flops 50723328 | bytes 7480320 | tf_op jit(solution)/shard_map/rkge,krje->krgj/dot_general | solution.py:178
  118.5 0.5 fusion.8
  119.1 4.6 %fusion.5 = bf16[24,8,8,128]{3,2,1,0:T(8,128)(2,1)S(1)} fusion(bf16[8,24,128,128]{3,2,1,0:T(8,128)(2,1)} %param.20, f32[24,8,128]{2,1,0:T(8,128)S(1)} %bitcast.58, f32[24,8,8]{2,1,0:T(8,128)S(1)} %copy.43, f32[8,24,8,128]{3,2,1,0:T(8,128)S(1)} %get-tuple-element.60, f32[8,24,8]{2,1,0:T(8,128)S(1)} %get-tuple-element.58, f32[8,24,8]{2,1,0:T(8,128)S(1)} %max.3, ...), kind=kOutput, calls=%fused_computation.4 | convolution fusion | flops 51707904 | bytes 7590912 | tf_op jit(solution)/shard_map/krgj,krje->rkge/dot_general | solution.py:187
  124.1 15.5 %all_to_all.40 = bf16[16,24,512]{2,1,0:T(8,128)(2,1)S(1)} all-to-all(bf16[16,24,512]{2,1,0:T(8,128)(2,1)S(1)} %bitcast.54), channel_id=1, replica_groups=mesh['rep'=2,'z'=4,'y'=2,'core'=2] {'z','y','core'}, dimensions={0} | all-to-all | bytes 786432 | tf_op jit(solution)/shard_map/all_to_all | solution.py:314
  139.8 1.6 collective-permute-done.17.refs_1_
  141.4 0.8 copy-done.6
  142.2 3.4 %shard_map.122 = bf16[384,512]{1,0:T(8,128)(2,1)} custom-call(s32[16]{0:T(128)} %stack.43.places, bf16[384,512]{1,0:T(8,128)(2,1)} %bitcast.47, bf16[384,512]{1,0:T(8,128)(2,1)} %copy-done.6, bf16[512,8192]{1,0:T(8,128)(2,1)} %refs_2_.3, bf16[512,8192]{1,0:T(8,128)(2,1)} %collective-permute-done.18.refs_9_.refs_10_.refs_11_.refs_12_.refs_13_.refs_14_.refs_15_.refs_3_), custom_call_target="tpu_custom_call" | custom-call | flops 1 | bytes 1 | tf_op jit(solution)/shard_map/pallas_call | solution.py:156
  145.6 0.6 collective-permute-start.21
  146.2 7.5 %shard_map.121 = (bf16[384,512]{1,0:T(8,128)(2,1)}, bf16[384,512]{1,0:T(8,128)(2,1)}, bf16[384,512]{1,0:T(8,128)(2,1)}, bf16[384,512]{1,0:T(8,128)(2,1)}, bf16[3...) custom-call(s32[16]{0:T(128)} %stack.43.places, bf16[384,512]{1,0:T(8,128)(2,1)} %bitcast.48, ...), custom_call_target="tpu_custom_call" | custom-call | flops 1 | bytes 1 | tf_op jit(solution)/shard_map/pallas_call | solution.py:156
  153.7 1.5 collective-permute-start.20
  155.2 2.1 %collective-permute-done.21 = bf16[384,512]{1,0:T(8,128)(2,1)S(1)} collective-permute-done((bf16[384,512]{1,0:T(8,128)(2,1)}, bf16[384,512]{1,0:T(8,128)(2,1)S(1)}, u32[]{:S(2)}, u32[]{:S(2)}) %collective-permute-start.21) | collective-permute-done | bytes 393248 | tf_op jit(solution)/shard_map/ppermute | solution.py:194
  157.3 1.1 add_convert_fusion.3
  158.4 3.1 %collective-permute-start.22 = (bf16[384,512]{1,0:T(8,128)(2,1)S(1)}, bf16[384,512]{1,0:T(8,128)(2,1)S(1)}, u32[]{:S(2)}, u32[]{:S(2)}) collective-permute-start(bf16[384,512]{1,0:T(8,128)(2,1)S(1)} %add_convert_fusion.3), channel_id=1, source_target_pairs={{0,4},{4,8},{1,5},{5,9},{2,6},{6,10},{3,7},{7,11},{16,20},{20,24},... | collective-permute-start | bytes 1179656 | tf_op jit(solution)/shard_map/ppermute | solution.py:238
  161.4 0.6 collective-permute-start.24
  162.1 0.7 collective-permute-start.25
  162.7 1.5 collective-permute-start.19
  164.3 1.7 collective-permute-done.20
  165.9 3.3 %collective-permute-done.22 = bf16[384,512]{1,0:T(8,128)(2,1)S(1)} collective-permute-done((bf16[384,512]{1,0:T(8,128)(2,1)S(1)}, bf16[384,512]{1,0:T(8,128)(2,1)S(1)}, u32[]{:S(2)}, u32[]{:S(2)}) %collective-permute-start.22) | collective-permute-done | bytes 393248 | tf_op jit(solution)/shard_map/ppermute | solution.py:238
  169.2 1.1 add_convert_fusion.2
  170.4 2.5 %collective-permute-start.23 = (bf16[384,512]{1,0:T(8,128)(2,1)S(1)}, bf16[384,512]{1,0:T(8,128)(2,1)S(1)}, u32[]{:S(2)}, u32[]{:S(2)}) collective-permute-start(bf16[384,512]{1,0:T(8,128)(2,1)S(1)} %add_convert_fusion.2), channel_id=1, source_target_pairs={{0,4},{4,8},{8,12},{12,0},{1,5},{5,9},{9,13},{13,1},{2,6},{6,10},{... | collective-permute-start | bytes 1179656 | tf_op jit(solution)/shard_map/ppermute | solution.py:194
  172.9 1.5 collective-permute-done.24
  174.4 1.1 add_convert_fusion.1
  175.5 2.2 %collective-permute-start.26 = (bf16[384,512]{1,0:T(8,128)(2,1)S(1)}, bf16[384,512]{1,0:T(8,128)(2,1)S(1)}, u32[]{:S(2)}, u32[]{:S(2)}) collective-permute-start(bf16[384,512]{1,0:T(8,128)(2,1)S(1)} %add_convert_fusion.1), channel_id=1, source_target_pairs={{0,12},{4,0},{8,4},{12,8},{1,13},{5,1},{9,5},{13,9},{2,14},{6,2},{... | collective-permute-start | bytes 1179656 | tf_op jit(solution)/shard_map/ppermute | solution.py:194
  177.7 4.6 %collective-permute-done.19 = bf16[384,512]{1,0:T(8,128)(2,1)S(1)} collective-permute-done((bf16[384,512]{1,0:T(8,128)(2,1)}, bf16[384,512]{1,0:T(8,128)(2,1)S(1)}, u32[]{:S(2)}, u32[]{:S(2)}) %collective-permute-start.19) | collective-permute-done | bytes 393248 | tf_op jit(solution)/shard_map/ppermute | solution.py:194
  182.3 2.0 %collective-permute-done.23 = bf16[384,512]{1,0:T(8,128)(2,1)S(1)} collective-permute-done((bf16[384,512]{1,0:T(8,128)(2,1)S(1)}, bf16[384,512]{1,0:T(8,128)(2,1)S(1)}, u32[]{:S(2)}, u32[]{:S(2)}) %collective-permute-start.23) | collective-permute-done | bytes 393248 | tf_op jit(solution)/shard_map/ppermute | solution.py:194
  184.3 5.9 %collective-permute-done.26 = bf16[384,512]{1,0:T(8,128)(2,1)S(1)} collective-permute-done((bf16[384,512]{1,0:T(8,128)(2,1)S(1)}, bf16[384,512]{1,0:T(8,128)(2,1)S(1)}, u32[]{:S(2)}, u32[]{:S(2)}) %collective-permute-start.26) | collective-permute-done | bytes 393248 | tf_op jit(solution)/shard_map/ppermute | solution.py:194
  190.1 1.9 %add_convert_fusion = bf16[384,512]{1,0:T(8,128)(2,1)} fusion(bf16[384,512]{1,0:T(8,128)(2,1)S(1)} %collective-permute-done.26, bf16[384,512]{1,0:T(8,128)(2,1)S(1)} %collective-permute-done.23, bf16[384,512]{1,0:T(8,128)(2,1)S(1)} %collective-permute-done.19, bf16[384,512]{1,0:T(8,128)(2,1)} %get-tuple-element.47), kind=kLoop, calls=%fused_computation.5 | loop fusion | flops 1572864 | bytes 1966080 | tf_op jit(solution)/shard_map/convert_element_type | solution.py:337
  (62 shorter events, 1.7 us)
Async XLA Ops:
  0.0 6.9 %copy-start = (bf16[1,8192,64]{1,2,0:T(8,128)(2,1)S(1)}, bf16[1,8192,64]{1,2,0:T(8,128)(2,1)}, u32[]{:S(2)}) copy-start(bf16[1,8192,64]{1,2,0:T(8,128)(2,1)} %param.18) | copy-start | bytes 3145732
  0.0 46.2 %collective-permute-start.9 = (bf16[8192,512]{1,0:T(8,128)(2,1)}, bf16[8192,512]{1,0:T(8,128)(2,1)}, u32[]{:S(2)}, u32[]{:S(2)}) collective-permute-start(bf16[8192,512]{1,0:T(8,128)(2,1)} %refs_7_.4), channel_id=1, source_target_pairs={{0,1},{1,0},{2,3},{3,2},{4,5},{5,4},{6,7},{7,6},{8,9},{9,8},{10,11... | collective-permute-start | bytes 25165832 | tf_op jit(solution)/shard_map/ppermute | solution.py:194
  0.5 25.8 %collective-permute-start = (bf16[384,512]{1,0:T(8,128)(2,1)}, bf16[384,512]{1,0:T(8,128)(2,1)S(1)}, u32[]{:S(2)}, u32[]{:S(2)}) collective-permute-start(bf16[384,512]{1,0:T(8,128)(2,1)} %refs_0_.1), channel_id=1, source_target_pairs={{0,4},{4,8},{8,12},{12,0},{1,5},{5,9},{9,13},{13,1},{2,6},{6,10},{... | collective-permute-start | bytes 1179656 | tf_op jit(solution)/shard_map/ppermute | solution.py:194
  3.1 23.2 %collective-permute-start.1 = (bf16[384,512]{1,0:T(8,128)(2,1)}, bf16[384,512]{1,0:T(8,128)(2,1)S(1)}, u32[]{:S(2)}, u32[]{:S(2)}) collective-permute-start(bf16[384,512]{1,0:T(8,128)(2,1)} %refs_0_.1), channel_id=1, source_target_pairs={{0,2},{2,0},{1,3},{3,1},{4,6},{6,4},{5,7},{7,5},{8,10},{10,8},{9,1... | collective-permute-start | bytes 1179656 | tf_op jit(solution)/shard_map/ppermute | solution.py:194
  4.6 20.4 %collective-permute-start.4 = (bf16[384,512]{1,0:T(8,128)(2,1)}, bf16[384,512]{1,0:T(8,128)(2,1)S(1)}, u32[]{:S(2)}, u32[]{:S(2)}) collective-permute-start(bf16[384,512]{1,0:T(8,128)(2,1)} %refs_0_.1), channel_id=1, source_target_pairs={{0,12},{4,0},{8,4},{12,8},{1,13},{5,1},{9,5},{13,9},{2,14},{6,2},{... | collective-permute-start | bytes 1179656 | tf_op jit(solution)/shard_map/ppermute | solution.py:194
  6.9 19.4 %collective-permute-start.2 = (bf16[1,64,8192]{2,1,0:T(8,128)(2,1)}, bf16[1,64,8192]{2,1,0:T(8,128)(2,1)S(1)}, u32[]{:S(2)}, u32[]{:S(2)}) collective-permute-start(bf16[1,64,8192]{2,1,0:T(8,128)(2,1)} %bitcast.37), channel_id=1, source_target_pairs={{0,1},{1,0},{2,3},{3,2},{4,5},{5,4},{6,7},{7,6},{8,9},{9,8},{10,11... | collective-permute-start | bytes 3145736 | tf_op jit(solution)/shard_map/ppermute | solution.py:194
  8.2 34.0 %all-to-all-start = ((bf16[32,16,512]{2,0,1:T(8,128)(2,1)}), bf16[32,16,512]{2,0,1:T(8,128)(2,1)S(1)}, u32[]{:S(2)}, u32[]{:S(2)}) async-start(bf16[32,16,512]{2,0,1:T(8,128)(2,1)} %copy.36), calls=%async_computation | async-start | bytes 1048576 | tf_op jit(solution)/shard_map/all_to_all | solution.py:290
  25.0 21.3 %copy-start.11 = (bf16[384,512]{1,0:T(8,128)(2,1)}, bf16[384,512]{1,0:T(8,128)(2,1)S(1)}, u32[]{:S(2)}) copy-start(bf16[384,512]{1,0:T(8,128)(2,1)S(1)} %collective-permute-done.4.refs_3_) | copy-start | bytes 1179652
  25.0 15.4 %collective-permute-start.7 = (bf16[384,512]{1,0:T(8,128)(2,1)S(1)}, bf16[384,512]{1,0:T(8,128)(2,1)S(1)}, u32[]{:S(2)}, u32[]{:S(2)}) collective-permute-start(bf16[384,512]{1,0:T(8,128)(2,1)S(1)} %collective-permute-done.4.refs_3_), channel_id=1, source_target_pairs={{8,4},{4,0},{9,5},{5,1},{10,6},{6,2},{11,7},{7,3},{24,20},{20,16},... | collective-permute-start | bytes 1179656 | tf_op jit(solution)/shard_map/ppermute | solution.py:224
  26.3 20.0 %copy-start.9 = (bf16[384,512]{1,0:T(8,128)(2,1)}, bf16[384,512]{1,0:T(8,128)(2,1)S(1)}, u32[]{:S(2)}) copy-start(bf16[384,512]{1,0:T(8,128)(2,1)S(1)} %collective-permute-done.refs_2_) | copy-start | bytes 1179652
  26.3 20.0 %copy-start.10 = (bf16[384,512]{1,0:T(8,128)(2,1)}, bf16[384,512]{1,0:T(8,128)(2,1)S(1)}, u32[]{:S(2)}) copy-start(bf16[384,512]{1,0:T(8,128)(2,1)S(1)} %collective-permute-done.1.refs_1_) | copy-start | bytes 1179652
  26.3 20.0 %copy-start.2 = (bf16[1,64,8192]{2,1,0:T(8,128)(2,1)}, bf16[1,64,8192]{2,1,0:T(8,128)(2,1)S(1)}, u32[]{:S(2)}) copy-start(bf16[1,64,8192]{2,1,0:T(8,128)(2,1)S(1)} %collective-permute-done.2.refs_16_.refs_17_.refs_18_.refs_19_) | copy-start | bytes 3145732
  26.3 14.8 %collective-permute-start.6 = (bf16[384,512]{1,0:T(8,128)(2,1)S(1)}, bf16[384,512]{1,0:T(8,128)(2,1)}, u32[]{:S(2)}, u32[]{:S(2)}) collective-permute-start(bf16[384,512]{1,0:T(8,128)(2,1)S(1)} %collective-permute-done.refs_2_), channel_id=1, source_target_pairs={{4,8},{8,12},{5,9},{9,13},{6,10},{10,14},{7,11},{11,15},{20,24},{2... | collective-permute-start | bytes 1179656 | tf_op jit(solution)/shard_map/ppermute | solution.py:222
  27.7 14.4 %collective-permute-start.3 = (bf16[384,512]{1,0:T(8,128)(2,1)S(1)}, bf16[384,512]{1,0:T(8,128)(2,1)}, u32[]{:S(2)}, u32[]{:S(2)}) collective-permute-start(bf16[384,512]{1,0:T(8,128)(2,1)S(1)} %collective-permute-done.refs_2_), channel_id=1, source_target_pairs={{0,2},{2,0},{1,3},{3,1},{4,6},{6,4},{5,7},{7,5},{8,10},{10,8},{9,1... | collective-permute-start | bytes 1179656 | tf_op jit(solution)/shard_map/ppermute | solution.py:194
  28.4 24.4 %collective-permute-start.5 = (bf16[384,512]{1,0:T(8,128)(2,1)S(1)}, bf16[384,512]{1,0:T(8,128)(2,1)}, u32[]{:S(2)}, u32[]{:S(2)}) collective-permute-start(bf16[384,512]{1,0:T(8,128)(2,1)S(1)} %collective-permute-done.4.refs_3_), channel_id=1, source_target_pairs={{0,2},{2,0},{1,3},{3,1},{4,6},{6,4},{5,7},{7,5},{8,10},{10,8},{9,1... | collective-permute-start | bytes 1179656 | tf_op jit(solution)/shard_map/ppermute | solution.py:194
  40.3 0.7 copy-start.12
  42.1 10.7 %copy-start.5 = (bf16[384,512]{1,0:T(8,128)(2,1)}, bf16[384,512]{1,0:T(8,128)(2,1)S(1)}, u32[]{:S(2)}) copy-start(bf16[384,512]{1,0:T(8,128)(2,1)S(1)} %broadcast_select_fusion.refs_2_) | copy-start | bytes 1179652
  42.1 21.4 %copy-start.4 = (bf16[32,16,512]{2,0,1:T(8,128)(2,1)}, bf16[32,16,512]{2,0,1:T(8,128)(2,1)S(1)}, u32[]{:S(2)}) copy-start(bf16[32,16,512]{2,0,1:T(8,128)(2,1)S(1)} %all-to-all-done) | copy-start | bytes 1572868
  42.2 14.0 %collective-permute-start.8 = (bf16[384,512]{1,0:T(8,128)(2,1)S(1)}, bf16[384,512]{1,0:T(8,128)(2,1)}, u32[]{:S(2)}, u32[]{:S(2)}) collective-permute-start(bf16[384,512]{1,0:T(8,128)(2,1)S(1)} %broadcast_select_fusion.refs_2_), channel_id=1, source_target_pairs={{0,2},{2,0},{1,3},{3,1},{4,6},{6,4},{5,7},{7,5},{8,10},{10,8},{9,1... | collective-permute-start | bytes 1179656 | tf_op jit(solution)/shard_map/ppermute | solution.py:194
  56.2 43.8 %copy-start.13 = (bf16[24,1024]{1,0:T(8,128)(2,1)S(1)}, bf16[24,1024]{1,0:T(8,128)(2,1)}, u32[]{:S(2)}) copy-start(bf16[24,1024]{1,0:T(8,128)(2,1)} %param.21) | copy-start | bytes 147460
  56.2 43.8 %copy-start.14 = (bf16[24,1024]{1,0:T(8,128)(2,1)S(1)}, bf16[24,1024]{1,0:T(8,128)(2,1)}, u32[]{:S(2)}) copy-start(bf16[24,1024]{1,0:T(8,128)(2,1)} %param.22) | copy-start | bytes 147460
  56.2 43.9 %copy-start.15 = (s32[24]{0:T(128)S(1)}, s32[24]{0:T(128)}, u32[]{:S(2)}) copy-start(s32[24]{0:T(128)} %param.15) | copy-start | bytes 292
  63.5 18.5 %collective-permute-start.13 = (f32[384,512]{1,0:T(8,128)}, f32[384,512]{1,0:T(8,128)S(1)}, u32[]{:S(2)}, u32[]{:S(2)}) collective-permute-start(f32[384,512]{1,0:T(8,128)} %get-tuple-element.41), channel_id=1, source_target_pairs={{0,1},{1,0},{2,3},{3,2},{4,5},{5,4},{6,7},{7,6},{8,9},{9,8},{10,11... | collective-permute-start | bytes 2359304 | tf_op jit(solution)/shard_map/ppermute | solution.py:194
  63.5 14.3 %collective-permute-start.11 = (bf16[512,512]{1,0:T(8,128)(2,1)S(1)}, bf16[512,512]{1,0:T(8,128)(2,1)S(1)}, u32[]{:S(2)}, u32[]{:S(2)}) collective-permute-start(bf16[512,512]{1,0:T(8,128)(2,1)S(1)} %bitcast.51), channel_id=1, source_target_pairs={{0,16},{16,0},{1,17},{17,1},{2,18},{18,2},{3,19},{19,3},{4,20},{20... | collective-permute-start | bytes 1572872 | tf_op jit(solution)/shard_map/ppermute | solution.py:294
  65.1 1.5 collective-permute-start.10
  77.9 13.1 %copy-start.8 = (bf16[512,512]{1,0:T(8,128)(2,1)}, bf16[512,512]{1,0:T(8,128)(2,1)S(1)}, u32[]{:S(2)}) copy-start(bf16[512,512]{1,0:T(8,128)(2,1)S(1)} %collective-permute-done.11.up_other) | copy-start | bytes 1572868
  77.9 4.1 %collective-permute-start.12 = (bf16[192,128]{1,0:T(8,128)(2,1)S(1)}, bf16[192,128]{1,0:T(8,128)(2,1)S(1)}, u32[]{:S(2)}, u32[]{:S(2)}) collective-permute-start(bf16[192,128]{1,0:T(8,128)(2,1)S(1)} %add_convert_fusion.4), channel_id=1, source_target_pairs={{0,2},{2,0},{1,3},{3,1},{4,6},{6,4},{5,7},{7,5},{8,10},{10,8},{9,1... | collective-permute-start | bytes 147464 | tf_op jit(solution)/shard_map/ppermute | solution.py:194
  82.0 9.0 %copy-start.7 = (f32[384,512]{1,0:T(8,128)}, f32[384,512]{1,0:T(8,128)S(1)}, u32[]{:S(2)}) copy-start(f32[384,512]{1,0:T(8,128)S(1)} %collective-permute-done.13.received) | copy-start | bytes 2359300
  82.0 6.1 %collective-permute-start.14 = (bf16[192,128]{1,0:T(8,128)(2,1)S(1)}, bf16[192,128]{1,0:T(8,128)(2,1)S(1)}, u32[]{:S(2)}, u32[]{:S(2)}) collective-permute-start(bf16[192,128]{1,0:T(8,128)(2,1)S(1)} %add.217), channel_id=1, source_target_pairs={{0,4},{4,8},{8,12},{12,0},{1,5},{5,9},{9,13},{13,1},{2,6},{6,10},{... | collective-permute-start | bytes 147464 | tf_op jit(solution)/shard_map/ppermute | solution.py:194
  84.8 5.5 %collective-permute-start.15 = (bf16[192,128]{1,0:T(8,128)(2,1)S(1)}, bf16[192,128]{1,0:T(8,128)(2,1)S(1)}, u32[]{:S(2)}, u32[]{:S(2)}) collective-permute-start(bf16[192,128]{1,0:T(8,128)(2,1)S(1)} %add.217), channel_id=1, source_target_pairs={{0,8},{4,12},{8,0},{12,4},{1,9},{5,13},{9,1},{13,5},{2,10},{6,14},... | collective-permute-start | bytes 147464 | tf_op jit(solution)/shard_map/ppermute | solution.py:194
  84.9 5.4 %collective-permute-start.16 = (bf16[192,128]{1,0:T(8,128)(2,1)S(1)}, bf16[192,128]{1,0:T(8,128)(2,1)S(1)}, u32[]{:S(2)}, u32[]{:S(2)}) collective-permute-start(bf16[192,128]{1,0:T(8,128)(2,1)S(1)} %add.217), channel_id=1, source_target_pairs={{0,12},{4,0},{8,4},{12,8},{1,13},{5,1},{9,5},{13,9},{2,14},{6,2},{... | collective-permute-start | bytes 147464 | tf_op jit(solution)/shard_map/ppermute | solution.py:194
  94.6 46.8 %collective-permute-start.18 = (bf16[512,8192]{1,0:T(8,128)(2,1)}, bf16[512,8192]{1,0:T(8,128)(2,1)}, u32[]{:S(2)}, u32[]{:S(2)}) collective-permute-start(bf16[512,8192]{1,0:T(8,128)(2,1)} %refs_2_.3), channel_id=1, source_target_pairs={{0,1},{1,0},{2,3},{3,2},{4,5},{5,4},{6,7},{7,6},{8,9},{9,8},{10,11... | collective-permute-start | bytes 25165832 | tf_op jit(solution)/shard_map/ppermute | solution.py:194
  94.6 17.6 %all-to-all-start.1 = ((bf16[16,24,512]{2,1,0:T(8,128)(2,1)}), bf16[16,24,512]{2,1,0:T(8,128)(2,1)S(1)}, u32[]{:S(2)}, u32[]{:S(2)}) async-start(bf16[16,24,512]{2,1,0:T(8,128)(2,1)} %bitcast.55), calls=%async_computation.1 | async-start | bytes 786432 | tf_op jit(solution)/shard_map/all_to_all | solution.py:308
  139.7 1.7 copy-start.3
  139.7 1.7 collective-permute-start.17
  141.4 0.8 copy-start.6
  145.6 11.6 %collective-permute-start.21 = (bf16[384,512]{1,0:T(8,128)(2,1)}, bf16[384,512]{1,0:T(8,128)(2,1)S(1)}, u32[]{:S(2)}, u32[]{:S(2)}) collective-permute-start(bf16[384,512]{1,0:T(8,128)(2,1)} %shard_map.122), channel_id=1, source_target_pairs={{0,2},{2,0},{1,3},{3,1},{4,6},{6,4},{5,7},{7,5},{8,10},{10,8},{9,1... | collective-permute-start | bytes 1179656 | tf_op jit(solution)/shard_map/ppermute | solution.py:194
  146.2 45.8 %copy-start.1 = (bf16[1,8192,64]{1,2,0:T(8,128)(2,1)S(1)}, bf16[1,8192,64]{1,2,0:T(8,128)(2,1)}, u32[]{:S(2)}) copy-start(bf16[1,8192,64]{1,2,0:T(8,128)(2,1)} %param.18) | copy-start | bytes 3145732
  153.7 12.2 %collective-permute-start.20 = (bf16[384,512]{1,0:T(8,128)(2,1)}, bf16[384,512]{1,0:T(8,128)(2,1)S(1)}, u32[]{:S(2)}, u32[]{:S(2)}) collective-permute-start(bf16[384,512]{1,0:T(8,128)(2,1)} %get-tuple-element.51), channel_id=1, source_target_pairs={{0,2},{2,0},{1,3},{3,1},{4,6},{6,4},{5,7},{7,5},{8,10},{10,8},{9,1... | collective-permute-start | bytes 1179656 | tf_op jit(solution)/shard_map/ppermute | solution.py:194
  158.4 10.9 %collective-permute-start.22 = (bf16[384,512]{1,0:T(8,128)(2,1)S(1)}, bf16[384,512]{1,0:T(8,128)(2,1)S(1)}, u32[]{:S(2)}, u32[]{:S(2)}) collective-permute-start(bf16[384,512]{1,0:T(8,128)(2,1)S(1)} %add_convert_fusion.3), channel_id=1, source_target_pairs={{0,4},{4,8},{1,5},{5,9},{2,6},{6,10},{3,7},{7,11},{16,20},{20,24},... | collective-permute-start | bytes 1179656 | tf_op jit(solution)/shard_map/ppermute | solution.py:238
  161.4 12.9 %collective-permute-start.24 = (bf16[384,512]{1,0:T(8,128)(2,1)}, bf16[384,512]{1,0:T(8,128)(2,1)S(1)}, u32[]{:S(2)}, u32[]{:S(2)}) collective-permute-start(bf16[384,512]{1,0:T(8,128)(2,1)} %get-tuple-element.56), channel_id=1, source_target_pairs={{0,2},{2,0},{1,3},{3,1},{4,6},{6,4},{5,7},{7,5},{8,10},{10,8},{9,1... | collective-permute-start | bytes 1179656 | tf_op jit(solution)/shard_map/ppermute | solution.py:194
  162.1 12.3 %collective-permute-start.25 = (bf16[384,512]{1,0:T(8,128)(2,1)S(1)}, bf16[384,512]{1,0:T(8,128)(2,1)S(1)}, u32[]{:S(2)}, u32[]{:S(2)}) collective-permute-start(bf16[384,512]{1,0:T(8,128)(2,1)S(1)} %add_convert_fusion.3), channel_id=1, source_target_pairs={{12,8},{8,4},{13,9},{9,5},{14,10},{10,6},{15,11},{11,7},{28,24},{2... | collective-permute-start | bytes 1179656 | tf_op jit(solution)/shard_map/ppermute | solution.py:239
  162.7 19.5 %collective-permute-start.19 = (bf16[384,512]{1,0:T(8,128)(2,1)}, bf16[384,512]{1,0:T(8,128)(2,1)S(1)}, u32[]{:S(2)}, u32[]{:S(2)}) collective-permute-start(bf16[384,512]{1,0:T(8,128)(2,1)} %get-tuple-element.48), channel_id=1, source_target_pairs={{0,2},{2,0},{1,3},{3,1},{4,6},{6,4},{5,7},{7,5},{8,10},{10,8},{9,1... | collective-permute-start | bytes 1179656 | tf_op jit(solution)/shard_map/ppermute | solution.py:194
  170.4 13.9 %collective-permute-start.23 = (bf16[384,512]{1,0:T(8,128)(2,1)S(1)}, bf16[384,512]{1,0:T(8,128)(2,1)S(1)}, u32[]{:S(2)}, u32[]{:S(2)}) collective-permute-start(bf16[384,512]{1,0:T(8,128)(2,1)S(1)} %add_convert_fusion.2), channel_id=1, source_target_pairs={{0,4},{4,8},{8,12},{12,0},{1,5},{5,9},{9,13},{13,1},{2,6},{6,10},{... | collective-permute-start | bytes 1179656 | tf_op jit(solution)/shard_map/ppermute | solution.py:194
  175.5 14.6 %collective-permute-start.26 = (bf16[384,512]{1,0:T(8,128)(2,1)S(1)}, bf16[384,512]{1,0:T(8,128)(2,1)S(1)}, u32[]{:S(2)}, u32[]{:S(2)}) collective-permute-start(bf16[384,512]{1,0:T(8,128)(2,1)S(1)} %add_convert_fusion.1), channel_id=1, source_target_pairs={{0,12},{4,0},{8,4},{12,8},{1,13},{5,1},{9,5},{13,9},{2,14},{6,2},{... | collective-permute-start | bytes 1179656 | tf_op jit(solution)/shard_map/ppermute | solution.py:194
